TPU v7x, 32 devices: a whole 2x2x4 slice. The times are simulated.
32 devices in a mesh: dp: 4 (over y, x), seq: 4 (over z), qblk: 2 (over core).
Axes of the slice: x: 2, y: 2, z: 4, core: 2. Of those that a mesh axis runs over, the one named last changes fastest.
Arguments:
- tokens: bfloat16 [8, 2048, 1024], P('dp', ('seq', 'qblk')), may hold values from -6 to 6
- cotangent: bfloat16 [8, 2048, 1024], P('dp', ('seq', 'qblk')), may hold values from -6 to 6
- w_qkv: float32 [1024, 3072], P(('dp', 'seq'), 'qblk'), may hold values from -0.1875 to 0.1875
- w_out: float32 [1024, 1024], P(('dp', 'seq'), 'qblk'), may hold values from -6 to 6
- w_in: float32 [1024, 5248], P(('dp', 'seq'), 'qblk'), may hold values from -0.1875 to 0.1875
- w_ffn: float32 [1024, 2624], P(('dp', 'seq'), 'qblk'), may hold values from -0.125 to 0.125
- gains: float32 [2, 1024], P(None, ('dp', 'seq', 'qblk')), may hold values from 0.5 to 1.5
- first_qkv: float32 [1024, 3072], P(('dp', 'seq'), 'qblk'), may hold values from -80 to 80
- second_qkv: float32 [1024, 3072], P(('dp', 'seq'), 'qblk'), may hold values from 16.384 to 65.536
- first_out: float32 [1024, 1024], P(('dp', 'seq'), 'qblk'), may hold values from -6 to 6
- second_out: float32 [1024, 1024], P(('dp', 'seq'), 'qblk'), may hold values from 0.024 to 0.096
- first_in: float32 [1024, 5248], P(('dp', 'seq'), 'qblk'), may hold values from -32 to 32
- second_in: float32 [1024, 5248], P(('dp', 'seq'), 'qblk'), may hold values from 2.62144 to 10.48576
- first_ffn: float32 [1024, 2624], P(('dp', 'seq'), 'qblk'), may hold values from -56 to 56
- second_ffn: float32 [1024, 2624], P(('dp', 'seq'), 'qblk'), may hold values from 6.88128 to 27.8528
- first_gain: float32 [2, 1024], P(None, ('dp', 'seq', 'qblk')), may hold values from -112 to 112
- second_gain: float32 [2, 1024], P(None, ('dp', 'seq', 'qblk')), may hold values from 27.8528 to 111.4112
Outputs:
- block_out: bfloat16 [8, 2048, 1024], P('dp', ('seq', 'qblk'))
- grad_input: float32 [8, 2048, 1024], P('dp', ('seq', 'qblk'))
- first_qkv_new: float32 [1024, 3072], P(('dp', 'seq'), 'qblk')
- second_qkv_new: float32 [1024, 3072], P(('dp', 'seq'), 'qblk')
- w_qkv_new: float32 [1024, 3072], P(('dp', 'seq'), 'qblk')
- first_out_new: float32 [1024, 1024], P(('dp', 'seq'), 'qblk')
- second_out_new: float32 [1024, 1024], P(('dp', 'seq'), 'qblk')
- w_out_new: float32 [1024, 1024], P(('dp', 'seq'), 'qblk')
- first_in_new: float32 [1024, 5248], P(('dp', 'seq'), 'qblk')
- second_in_new: float32 [1024, 5248], P(('dp', 'seq'), 'qblk')
- w_in_new: float32 [1024, 5248], P(('dp', 'seq'), 'qblk')
- first_ffn_new: float32 [1024, 2624], P(('dp', 'seq'), 'qblk')
- second_ffn_new: float32 [1024, 2624], P(('dp', 'seq'), 'qblk')
- w_ffn_new: float32 [1024, 2624], P(('dp', 'seq'), 'qblk')
- first_gain_new: float32 [2, 1024], P(None, ('dp', 'seq', 'qblk'))
- second_gain_new: float32 [2, 1024], P(None, ('dp', 'seq', 'qblk'))
- gains_new: float32 [2, 1024], P(None, ('dp', 'seq', 'qblk'))
All inputs are finite; a program needn't handle non-finite values.
Results may differ from a plain program's by a relative error of at most 0.02.
Values may be sent and summed in bfloat16 or wider, within the bound.
A program may use at most 320 MiB of HBM per device.

v0:
```python
import jax
import jax.numpy as jnp
from jax import lax
from jax.sharding import PartitionSpec as P

D = 1024
H = 16
HD = 64
FF = 2624
STEP = 10
OUT_FAN = 1


EPS_NORM = 1e-05
ROPE_BASE = 160000.0
BETA_ONE = 0.9
BETA_TWO = 0.999
ADAM_EPS = 1e-08
WEIGHT_DECAY = 0.01
LR_FACTOR = 3.0
LR_GAIN = 1.0


def rotary_cols(values, places):
    half_dim = HD // 2
    inv_freq = ROPE_BASE ** (-2.0 * jnp.arange(half_dim, dtype=jnp.float32) / HD)
    angles = inv_freq[:, None] * places[None, :]
    cos_part = jnp.cos(angles)
    sin_part = jnp.sin(angles)
    lower_half = values[..., :half_dim, :]
    upper_half = values[..., half_dim:, :]
    return jnp.concatenate(
        [
            lower_half * cos_part - upper_half * sin_part,
            upper_half * cos_part + lower_half * sin_part,
        ],
        axis=-2,
    )


def norm_fwd(values, gain_row):
    row_mean = jnp.mean(values, axis=-1, keepdims=True)
    centered = values - row_mean
    row_var = jnp.mean(centered * centered, axis=-1, keepdims=True)
    inv_std = lax.rsqrt(row_var + EPS_NORM)
    normed = centered * inv_std
    return (normed, inv_std, (normed * gain_row).astype(jnp.bfloat16))


def norm_back(upstream, normed, inv_std, gain_row):
    scaled = upstream * gain_row
    return inv_std * (
        scaled
        - jnp.mean(scaled, axis=-1, keepdims=True)
        - normed * jnp.mean(scaled * normed, axis=-1, keepdims=True)
    )


def gated(gate_part, up_part):
    return jax.nn.gelu(gate_part, approximate=False) * up_part


def attend(block_in):
    q_rows, k_rows, v_rows = block_in
    scores = jnp.einsum(
        "hdq,hdk->hqk", q_rows, k_rows, preferred_element_type=jnp.float32
    ) * HD ** (-0.5)
    row_max = jnp.max(scores, axis=-1, keepdims=True)
    exp_scores = jnp.exp(scores - row_max)
    row_sum = jnp.sum(exp_scores, axis=-1, keepdims=True)
    probs_low = (exp_scores / row_sum).astype(jnp.bfloat16)
    attn_out = jnp.einsum("hqk,hdk->hdq", probs_low, v_rows, preferred_element_type=jnp.float32)
    return (attn_out.astype(jnp.bfloat16), row_max[..., 0], row_sum[..., 0])


def attend_back(block_in):
    q_rows, k_rows, v_rows, out_grad, row_max, row_sum = block_in
    scores = jnp.einsum(
        "hdq,hdk->hqk", q_rows, k_rows, preferred_element_type=jnp.float32
    ) * HD ** (-0.5)
    probs = jnp.exp(scores - row_max[..., None]) / row_sum[..., None]
    prob_grad = jnp.einsum("hdq,hdk->hqk", out_grad, v_rows, preferred_element_type=jnp.float32)
    inner = jnp.sum(probs * prob_grad, axis=-1, keepdims=True)
    score_grad = (probs * (prob_grad - inner)).astype(jnp.bfloat16)
    q_grad = jnp.einsum(
        "hqk,hdk->hdq", score_grad, k_rows, preferred_element_type=jnp.float32
    ) * HD ** (-0.5)
    k_grad = jnp.einsum(
        "hqk,hdq->hdk", score_grad, q_rows, preferred_element_type=jnp.float32
    ) * HD ** (-0.5)
    v_grad = jnp.einsum(
        "hqk,hdq->hdk", probs.astype(jnp.bfloat16), out_grad, preferred_element_type=jnp.float32
    )
    return (q_grad, k_grad, v_grad)


def adam_step(weight, grad_sum, moment, second, learn_rate, weight_decay):
    moment_new = BETA_ONE * moment + (1.0 - BETA_ONE) * grad_sum
    second_new = BETA_TWO * second + (1.0 - BETA_TWO) * grad_sum * grad_sum
    update = (
        moment_new
        / (1.0 - BETA_ONE**STEP)
        / (jnp.sqrt(second_new / (1.0 - BETA_TWO**STEP)) + ADAM_EPS)
    )
    return (moment_new, second_new, weight - learn_rate * (update + weight_decay * weight))


def on_device(
    tokens,
    cotangent,
    w_qkv,
    w_out,
    w_in,
    w_ffn,
    gains,
    first_qkv,
    second_qkv,
    first_out,
    second_out,
    first_in,
    second_in,
    first_ffn,
    second_ffn,
    first_gain,
    second_gain,
):
    n_seq = lax.axis_size("seq")
    n_blk = lax.axis_size("qblk")
    seq_count, tok_local, width = tokens.shape
    row_count = seq_count * tok_local
    half_cols = (
        lax.all_gather(w_qkv.astype(jnp.bfloat16), "qblk", axis=1, tiled=True),
        lax.all_gather(w_out.astype(jnp.bfloat16), "qblk", axis=1, tiled=True),
        lax.all_gather(w_in.astype(jnp.bfloat16), "qblk", axis=1, tiled=True),
        lax.all_gather(w_ffn.astype(jnp.bfloat16), "qblk", axis=1, tiled=True),
        lax.all_gather(gains.astype(jnp.bfloat16), "qblk", axis=1, tiled=True),
    )
    cols_qkv, cols_out, cols_in, cols_ffn, cols_gain = half_cols
    full_qkv, full_out, full_in, full_ffn, full_gain = (
        lax.all_gather(cols_qkv, ("dp", "seq"), axis=0, tiled=True),
        lax.all_gather(cols_out, ("dp", "seq"), axis=0, tiled=True),
        lax.all_gather(cols_in, ("dp", "seq"), axis=0, tiled=True),
        lax.all_gather(cols_ffn, ("dp", "seq"), axis=0, tiled=True),
        lax.all_gather(cols_gain, ("dp", "seq"), axis=1, tiled=True),
    )
    gain_rows = full_gain.astype(jnp.float32)
    qkv_four = full_qkv.reshape(width, 3, H, HD)
    out_three = full_out.reshape(H, HD, width)
    block_idx = lax.axis_index("qblk")
    place_ids = jnp.arange(n_seq * tok_local, dtype=jnp.int32)
    positions = (
        (place_ids // tok_local * n_blk + block_idx) * tok_local + place_ids % tok_local
    ).astype(jnp.float32)
    resid_in = tokens.astype(jnp.float32).reshape(row_count, width)
    normed_one, inv_one, attn_in = norm_fwd(resid_in, gain_rows[0])
    attn_seq = attn_in.reshape(seq_count, tok_local, width)
    proj_qkv = jnp.einsum(
        "std,dkhe->skhet", attn_seq, qkv_four, preferred_element_type=jnp.float32
    ).astype(jnp.bfloat16)
    by_heads = lax.all_to_all(proj_qkv, "seq", split_axis=2, concat_axis=4, tiled=True)
    q_rot = rotary_cols(by_heads[:, 0].astype(jnp.float32), positions).astype(jnp.bfloat16)
    k_rot = rotary_cols(by_heads[:, 1].astype(jnp.float32), positions).astype(jnp.bfloat16)
    v_local = by_heads[:, 2]
    k_all, v_all = (
        lax.all_gather(k_rot, "qblk", axis=3, tiled=True),
        lax.all_gather(v_local, "qblk", axis=3, tiled=True),
    )
    head_out, row_max, row_sum = lax.map(attend, (q_rot, k_all, v_all))
    attn_heads = lax.all_to_all(head_out, "seq", split_axis=3, concat_axis=1, tiled=True)
    resid_mid = resid_in + jnp.einsum(
        "shet,hed->std", attn_heads, out_three, preferred_element_type=jnp.float32
    ).reshape(row_count, width)
    normed_two, inv_two, ffn_in = norm_fwd(resid_mid, gain_rows[1])
    gate_up = jnp.dot(ffn_in, full_in, preferred_element_type=jnp.float32)
    gate_part = gate_up[:, :FF]
    up_part = gate_up[:, FF:]
    hidden = gated(gate_part, up_part).astype(jnp.bfloat16)
    block_out = (
        (resid_mid + jnp.einsum("tf,ef->te", hidden, full_ffn, preferred_element_type=jnp.float32))
        .astype(jnp.bfloat16)
        .reshape(tokens.shape)
    )
    grad_y = cotangent.astype(jnp.float32).reshape(row_count, width)
    grad_low = grad_y.astype(jnp.bfloat16)
    grad_ffn = jnp.einsum("te,tf->ef", grad_low, hidden, preferred_element_type=jnp.float32)
    hidden_grad = jnp.einsum("te,ef->tf", grad_low, full_ffn, preferred_element_type=jnp.float32)
    glu_pullback = jax.vjp(gated, gate_part, up_part)[1]
    gate_grad, up_grad = glu_pullback(hidden_grad)
    gate_up_grad = jnp.concatenate([gate_grad, up_grad], axis=-1).astype(jnp.bfloat16)
    grad_in = jnp.einsum("td,tf->df", ffn_in, gate_up_grad, preferred_element_type=jnp.float32)
    ffn_in_grad = jnp.einsum("tf,df->td", gate_up_grad, full_in, preferred_element_type=jnp.float32)
    gain_two_grad = jnp.sum(ffn_in_grad * normed_two, axis=0)
    mid_grad = grad_y + norm_back(ffn_in_grad, normed_two, inv_two, gain_rows[1])
    mid_low = mid_grad.astype(jnp.bfloat16).reshape(seq_count, tok_local, width)
    grad_out = jnp.einsum(
        "shet,std->hed", attn_heads, mid_low, preferred_element_type=jnp.float32
    ).reshape(width, width)
    attn_grad = jnp.einsum(
        "std,hed->shet", mid_low, out_three, preferred_element_type=jnp.float32
    ).astype(jnp.bfloat16)
    heads_grad = lax.all_to_all(attn_grad, "seq", split_axis=1, concat_axis=3, tiled=True)
    q_grad, k_part, v_part = lax.map(
        attend_back, (q_rot, k_all, v_all, heads_grad, row_max, row_sum)
    )
    k_grad, v_grad = (
        lax.psum_scatter(
            k_part.astype(jnp.bfloat16), "qblk", scatter_dimension=3, tiled=True
        ).astype(jnp.float32),
        lax.psum_scatter(
            v_part.astype(jnp.bfloat16), "qblk", scatter_dimension=3, tiled=True
        ).astype(jnp.float32),
    )
    rot_pullback = jax.vjp(lambda values: rotary_cols(values, positions), q_grad)[1]
    q_pre = rot_pullback(q_grad)[0]
    k_pre = rot_pullback(k_grad)[0]
    qkv_heads_grad = jnp.stack([q_pre, k_pre, v_grad], axis=1).astype(jnp.bfloat16)
    qkv_grad = lax.all_to_all(qkv_heads_grad, "seq", split_axis=4, concat_axis=2, tiled=True)
    grad_qkv = jnp.einsum(
        "std,skhet->dkhe", attn_seq, qkv_grad, preferred_element_type=jnp.float32
    ).reshape(width, 3 * width)
    in_grad = jnp.einsum(
        "skhet,dkhe->std", qkv_grad, qkv_four, preferred_element_type=jnp.float32
    ).reshape(row_count, width)
    gain_one_grad = jnp.sum(in_grad * normed_one, axis=0)
    grad_x = mid_grad + norm_back(in_grad, normed_one, inv_one, gain_rows[0])
    gain_grads = jnp.stack([gain_one_grad, gain_two_grad])
    rows_qkv, rows_out, rows_in, rows_ffn, rows_gain = (
        lax.psum_scatter(grad_qkv, ("dp", "seq"), scatter_dimension=0, tiled=True),
        lax.psum_scatter(grad_out, ("dp", "seq"), scatter_dimension=0, tiled=True),
        lax.psum_scatter(grad_in, ("dp", "seq"), scatter_dimension=0, tiled=True),
        lax.psum_scatter(grad_ffn, ("dp", "seq"), scatter_dimension=0, tiled=True),
        lax.psum_scatter(gain_grads, ("dp", "seq"), scatter_dimension=1, tiled=True),
    )
    sum_qkv, sum_out, sum_in, sum_ffn, sum_gain = (
        lax.psum_scatter(
            rows_qkv.astype(jnp.bfloat16), "qblk", scatter_dimension=1, tiled=True
        ).astype(jnp.float32),
        lax.psum_scatter(
            rows_out.astype(jnp.bfloat16), "qblk", scatter_dimension=1, tiled=True
        ).astype(jnp.float32),
        lax.psum_scatter(
            rows_in.astype(jnp.bfloat16), "qblk", scatter_dimension=1, tiled=True
        ).astype(jnp.float32),
        lax.psum_scatter(
            rows_ffn.astype(jnp.bfloat16), "qblk", scatter_dimension=1, tiled=True
        ).astype(jnp.float32),
        lax.psum_scatter(
            rows_gain.astype(jnp.bfloat16), "qblk", scatter_dimension=1, tiled=True
        ).astype(jnp.float32),
    )
    new_qkv = adam_step(
        w_qkv, sum_qkv, first_qkv, second_qkv, LR_FACTOR * D ** (-0.5), WEIGHT_DECAY
    )
    new_out = adam_step(
        w_out, sum_out, first_out, second_out, LR_FACTOR * OUT_FAN ** (-0.5), WEIGHT_DECAY
    )
    new_in = adam_step(w_in, sum_in, first_in, second_in, LR_FACTOR * D ** (-0.5), WEIGHT_DECAY)
    new_ffn = adam_step(
        w_ffn, sum_ffn, first_ffn, second_ffn, LR_FACTOR * FF ** (-0.5), WEIGHT_DECAY
    )
    new_gain = adam_step(gains, sum_gain, first_gain, second_gain, LR_GAIN, 0.0)
    return (
        block_out,
        grad_x.reshape(tokens.shape),
        new_qkv[0],
        new_qkv[1],
        new_qkv[2],
        new_out[0],
        new_out[1],
        new_out[2],
        new_in[0],
        new_in[1],
        new_in[2],
        new_ffn[0],
        new_ffn[1],
        new_ffn[2],
        new_gain[0],
        new_gain[1],
        new_gain[2],
    )


def solution(mesh):
    placed = (
        P("dp", ("seq", "qblk"), None),
        P("dp", ("seq", "qblk"), None),
        P(("dp", "seq"), "qblk"),
        P(("dp", "seq"), "qblk"),
        P(("dp", "seq"), "qblk"),
        P(("dp", "seq"), "qblk"),
        P(None, ("dp", "seq", "qblk")),
        P(("dp", "seq"), "qblk"),
        P(("dp", "seq"), "qblk"),
        P(("dp", "seq"), "qblk"),
        P(("dp", "seq"), "qblk"),
        P(("dp", "seq"), "qblk"),
        P(("dp", "seq"), "qblk"),
        P(("dp", "seq"), "qblk"),
        P(("dp", "seq"), "qblk"),
        P(None, ("dp", "seq", "qblk")),
        P(None, ("dp", "seq", "qblk")),
    )
    return jax.shard_map(
        on_device,
        mesh=mesh,
        in_specs=placed,
        out_specs=(
            P("dp", ("seq", "qblk"), None),
            P("dp", ("seq", "qblk"), None),
            P(("dp", "seq"), "qblk"),
            P(("dp", "seq"), "qblk"),
            P(("dp", "seq"), "qblk"),
            P(("dp", "seq"), "qblk"),
            P(("dp", "seq"), "qblk"),
            P(("dp", "seq"), "qblk"),
            P(("dp", "seq"), "qblk"),
            P(("dp", "seq"), "qblk"),
            P(("dp", "seq"), "qblk"),
            P(("dp", "seq"), "qblk"),
            P(("dp", "seq"), "qblk"),
            P(("dp", "seq"), "qblk"),
            P(None, ("dp", "seq", "qblk")),
            P(None, ("dp", "seq", "qblk")),
            P(None, ("dp", "seq", "qblk")),
        ),
        check_vma=False,
    )
```

profile of v0, /device:TPU:0, one launch (start us, length us, event | category | flops | bytes accessed | tf_op | source)
XLA Modules:
  0.0 2049.5 jit_solution(12313566794831430145)
XLA Ops:
  13.2 42.3 %all-gather.2 = bf16[16,64,2]{1,2,0:T(2,128)(2,1)S(1)} all-gather(bf16[1,64,2]{1,2,0:T(2,128)(2,1)S(1)} %reshape.251), channel_id=1, replica_groups=mesh['dp'=4,'seq'=4,'qblk'=2] {'dp','seq'}, dimensions={0}, use_global_device_ids=true | all-gather | bytes 4352 | tf_op jit(solution)/shard_map/all_gather | solution.py:144
  60.5 47.4 %all-gather.12.cloned.1.call-done = bf16[1024,3072]{1,0:T(8,128)(2,1)} async-done(((bf16[64,3072]{1,0:T(8,128)(2,1)}), bf16[1024,3072]{1,0:T(8,128)(2,1)}) %all-gather.12.cloned.1.call-update) | async-done | bytes 6291472 | tf_op jit(solution)/shard_map/all_gather | solution.py:140
  123.7 73.5 %all_to_all.72 = bf16[2,3,16,64,256]{4,3,1,0,2:T(8,128)(2,1)S(1)} all-to-all(bf16[2,3,16,64,256]{4,3,1,0,2:T(8,128)(2,1)S(1)} %copy.170), channel_id=1, replica_groups=mesh['dp'=4,'seq'=4,'qblk'=2] {'seq'}, dimensions={2} | all-to-all | bytes 6291456 | tf_op jit(solution)/shard_map/all_to_all | solution.py:160
  231.0 88.2 %while.28 = (s32[]{:T(128)}, bf16[2,4,64,1024]{3,2,1,0:T(8,128)(2,1)}, f32[2,4,1024]{2,1,0:T(4,128)S(1)}, f32[2,4,1024]{2,1,0:T(4,128)S(1)}, bf16[2,4,64,2048]{3...) while((s32[]{:T(128)}, ...), condition=%wide.region_5.6_spmd, body=%wide.region_2.5_spmd.sunk | while | flops 2223235072 | bytes 112347256 | solution.py:168
  231.0 14.6 multiply_reduce_fusion.8
  245.6 14.1 fusion.156
  259.7 15.0 fusion.157
  274.8 14.6 multiply_reduce_fusion.8
  289.3 14.2 fusion.156
  303.5 15.7 fusion.157
  325.0 56.7 %all_to_all.73 = bf16[4,2,65536]{2,1,0:T(2,128)(2,1)S(1)} all-to-all(bf16[4,2,65536]{2,1,0:T(2,128)(2,1)} %reshape.280), channel_id=1, replica_groups=mesh['dp'=4,'seq'=4,'qblk'=2] {'seq'}, dimensions={0} | all-to-all | bytes 2097152 | tf_op jit(solution)/shard_map/all_to_all | solution.py:169
  394.9 58.0 %all-gather.18.cloned.1.call-done = bf16[1024,5248]{1,0:T(8,128)(2,1)} async-done(((bf16[64,5248]{1,0:T(8,128)(2,1)}), bf16[1024,5248]{1,0:T(8,128)(2,1)}) %all-gather.18.cloned.1.call-update) | async-done | bytes 10747920 | tf_op jit(solution)/shard_map/all_gather | solution.py:142
  465.7 75.8 %all-gather.20.cloned.1.call-done = bf16[1024,2624]{1,0:T(8,128)(2,1)} async-done(((bf16[64,2624]{1,0:T(8,128)(2,1)}), bf16[1024,2624]{1,0:T(8,128)(2,1)}) %all-gather.20.cloned.1.call-update) | async-done | bytes 5373968 | tf_op jit(solution)/shard_map/all_gather | solution.py:143
  541.5 20.0 add_convert_fusion
  566.2 13.9 multiply_reduce_fusion.2
  590.0 25.3 %all-to-all-done.2 = bf16[2,16,64,256]{3,2,0,1:T(8,128)(2,1)S(1)} async-done(((bf16[2,16,64,256]{3,2,0,1:T(8,128)(2,1)}), bf16[2,16,64,256]{3,2,0,1:T(8,128)(2,1)S(1)}, u32[]{:S(2)}, u32[]{:S(2)}) %all-to-all-start.2) | async-done | bytes 1048608 | tf_op jit(solution)/shard_map/all_to_all | solution.py:201
  618.9 203.4 %while.29 = (s32[]{:T(128)}, f32[2,4,64,1024]{3,2,1,0:T(8,128)}, bf16[2,4,64,2048]{3,2,1,0:T(8,128)(2,1)}, bf16[2,4,64,2048]{3,2,1,0:T(8,128)(2,1)}, bf16[2,4,64...) while((s32[]{:T(128)}, f32[2,4,64,1024]{3,2,1,0:T(8,128)}, ...), condition=%wide.region_12.13_spmd, body=%wide.region_10.12_spmd.sunk | while | flops 5444988928 | bytes 266474640 | solution.py:202
  619.1 14.5 fusion.166
  633.6 23.0 %multiply_reduce_fusion.9 = (f32[4,1024]{1,0:T(4,128)S(1)}, f32[4,1024,2048]{2,1,0:T(8,128)}) fusion(f32[4,1024,2048]{2,1,0:T(8,128)} %fusion.166, f32[4,1024]{1,0:T(4,128)S(1)} %get-tuple-element.418, f32[4,1024]{1,0:T(4,128)S(1)} %get-tuple-element.419, bf16[2,4,64,2048]{3,2,1,0:T(8,128)(2,1)S(1)} %get-tuple-element.472, s32[]{:T(128)S(6)} %copy.237, ...), kind=kOutput, calls=%fused_computation.21.clone.1 | convolution fusion | flops 1115680768 | bytes 68731904 | tf_op jit(solution)/shard_map/while/body/eval_jaxpr/hdq,hdk->hqk/dot_general | solution.py:78
  656.6 27.4 %multiply_convert_fusion.7 = bf16[4,1024,2048]{2,1,0:T(8,128)(2,1)} fusion(f32[4,1024,2048]{2,1,0:T(8,128)} %get-tuple-element.420, f32[4,1024,2048]{2,1,0:T(8,128)} %fusion.166, f32[4,1024]{1,0:T(4,128)S(1)} %get-tuple-element.421), kind=kLoop, calls=%fused_computation.20.clone.1 | loop fusion | flops 25165824 | bytes 83902464 | tf_op jit(solution)/shard_map/while/body/eval_jaxpr/convert_element_type | solution.py:84
  706.0 14.6 fusion.169
  720.5 14.4 fusion.166
  734.9 23.0 %multiply_reduce_fusion.9 = (f32[4,1024]{1,0:T(4,128)S(1)}, f32[4,1024,2048]{2,1,0:T(8,128)}) fusion(f32[4,1024,2048]{2,1,0:T(8,128)} %fusion.166, f32[4,1024]{1,0:T(4,128)S(1)} %get-tuple-element.418, f32[4,1024]{1,0:T(4,128)S(1)} %get-tuple-element.419, bf16[2,4,64,2048]{3,2,1,0:T(8,128)(2,1)S(1)} %get-tuple-element.472, s32[]{:T(128)S(6)} %copy.237, ...), kind=kOutput, calls=%fused_computation.21.clone.1 | convolution fusion | flops 1115680768 | bytes 68731904 | tf_op jit(solution)/shard_map/while/body/eval_jaxpr/hdq,hdk->hqk/dot_general | solution.py:78
  757.9 27.4 %multiply_convert_fusion.7 = bf16[4,1024,2048]{2,1,0:T(8,128)(2,1)} fusion(f32[4,1024,2048]{2,1,0:T(8,128)} %get-tuple-element.420, f32[4,1024,2048]{2,1,0:T(8,128)} %fusion.166, f32[4,1024]{1,0:T(4,128)S(1)} %get-tuple-element.421), kind=kLoop, calls=%fused_computation.20.clone.1 | loop fusion | flops 25165824 | bytes 83902464 | tf_op jit(solution)/shard_map/while/body/eval_jaxpr/convert_element_type | solution.py:84
  807.3 14.6 fusion.169
  841.4 30.2 %all-reduce.9.cloned.1.call-done = (bf16[2,4,64,2048]{2,1,0,3:T(4,128)(2,1)}, bf16[2,4,64,2048]{2,1,0,3:T(4,128)(2,1)}) async-done(((bf16[2,4,64,2048]{2,1,0,3:T(4,128)(2,1)}, bf16[2,4,64,2048]{2,1,0,3:T(4,128)(2,1)}), (bf16[2,4,64,2048]{2,1,0,3:T(4,128)(2,1)}, bf16[2,4,64,2048]{2,1,0,3:T(4,128)(2,1)})) %all-reduce.9.cloned.1.call-update) | async-done | bytes 4194320
  905.2 121.7 %all-to-all-done.3 = bf16[4,2,196608]{2,1,0:T(2,128)(2,1)S(1)} async-done(((bf16[4,2,196608]{2,1,0:T(2,128)(2,1)}), bf16[4,2,196608]{2,1,0:T(2,128)(2,1)S(1)}, u32[]{:S(2)}, u32[]{:S(2)}) %all-to-all-start.3) | async-done | bytes 3145760 | tf_op jit(solution)/shard_map/all_to_all | solution.py:217
  1032.2 15.3 copy.186
  1106.9 31.0 %reduce-scatter.37.cloned.1.call-done = f32[64,2]{1,0:T(8,128)} async-done(((f32[1024,2]{1,0:T(8,128)}), f32[64,2]{1,0:T(8,128)}) %reduce-scatter.37.cloned.1.call-update) | async-done | bytes 528
  1139.6 187.6 %reduce-scatter.33.cloned.1.call-done = f32[64,2624]{1,0:T(8,128)} async-done(((f32[1024,2624]{1,0:T(8,128)}), f32[64,2624]{1,0:T(8,128)}) %reduce-scatter.33.cloned.1.call-update) | async-done | bytes 671760
  1329.5 206.8 %reduce-scatter.21.cloned.1.call-done = f32[64,3072]{1,0:T(8,128)} async-done(((f32[1024,3072]{1,0:T(8,128)}), f32[64,3072]{1,0:T(8,128)}) %reduce-scatter.21.cloned.1.call-update) | async-done | bytes 786448 | tf_op jit(solution)/shard_map/reduce_scatter | solution.py:228
  1549.9 444.2 %reduce-scatter.29.cloned.1.call-done = f32[64,5248]{1,0:T(8,128)} async-done(((f32[1024,5248]{1,0:T(8,128)}), f32[64,5248]{1,0:T(8,128)}) %reduce-scatter.29.cloned.1.call-update) | async-done | bytes 1343504 | tf_op jit(solution)/shard_map/reduce_scatter | solution.py:230
  (273 shorter events, 336.5 us)
Async XLA Ops:
  7.2 100.7 %all-gather.12.cloned.1.call-start = ((), (), s32[]{:S(2)}) async-start(), calls=%async_computation.14 | async-start | bytes 6684672 | tf_op jit(solution)/shard_map/all_gather | solution.py:140
  10.6 213.0 %all-gather.22.cloned.1.call-start = ((), (), s32[]{:S(2)}) async-start(), calls=%async_computation.24 | async-start | bytes 3145728 | tf_op jit(solution)/shard_map/all_gather | solution.py:166
  57.6 58.9 %copy-start.44 = (f32[2,256]{1,0:T(2,128)}, f32[2,256]{1,0:T(2,128)S(1)}, u32[]{:S(2)}) copy-start(f32[2,256]{1,0:T(2,128)S(1)} %get-tuple-element.294) | copy-start | bytes 6148
  59.9 56.7 %copy-start.49 = (f32[2,256]{1,0:T(2,128)}, f32[2,256]{1,0:T(2,128)S(1)}, u32[]{:S(2)}) copy-start(f32[2,256]{1,0:T(2,128)S(1)} %get-tuple-element.292) | copy-start | bytes 6148
  60.5 56.1 %copy-start.42 = (f32[1,1024]{1,0:T(1,128)}, f32[1,1024]{1,0:T(1,128)S(1)}, u32[]{:S(2)}) copy-start(f32[1,1024]{1,0:T(1,128)S(1)} %get-tuple-element.288) | copy-start | bytes 12292
  60.5 56.1 %copy-start.5 = (bf16[2,256,1024]{2,1,0:T(8,128)(2,1)S(1)}, bf16[2,256,1024]{2,1,0:T(8,128)(2,1)}, u32[]{:S(2)}) copy-start(bf16[2,256,1024]{2,1,0:T(8,128)(2,1)} %param.21) | copy-start | bytes 3145732
  208.0 22.9 %all-gather.14.cloned.1.call-start = ((), (), s32[]{:S(2)}) async-start(), calls=%async_computation.15 | async-start | bytes 3145728 | tf_op jit(solution)/shard_map/all_gather | solution.py:165
  212.9 178.3 %all-gather.16.cloned.1.call-start = ((), (), s32[]{:S(2)}) async-start(), calls=%async_computation.16 | async-start | bytes 2228224 | tf_op jit(solution)/shard_map/all_gather | solution.py:141
  215.0 237.8 %all-gather.18.cloned.1.call-start = ((), (), s32[]{:S(2)}) async-start(), calls=%async_computation.17 | async-start | bytes 11419648 | tf_op jit(solution)/shard_map/all_gather | solution.py:142
  219.6 321.8 %all-gather.20.cloned.1.call-start = ((), (), s32[]{:S(2)}) async-start(), calls=%async_computation.18 | async-start | bytes 5849088 | tf_op jit(solution)/shard_map/all_gather | solution.py:143
  319.2 62.5 %copy-start.1 = (bf16[2,4,64,1024]{3,2,1,0:T(8,128)(2,1)}, bf16[2,4,64,1024]{3,2,1,0:T(8,128)(2,1)S(1)}, u32[]{:S(2)}) copy-start(bf16[2,4,64,1024]{3,2,1,0:T(8,128)(2,1)S(1)} %get-tuple-element.505) | copy-start | bytes 3145732
  391.2 61.7 %copy-start.34 = (f32[1,1024]{1,0:T(1,128)S(1)}, f32[1,1024]{1,0:T(1,128)}, u32[]{:S(2)}) copy-start(f32[1,1024]{1,0:T(1,128)} %get-tuple-element.287) | copy-start | bytes 12292
  394.5 185.7 %copy-start.3 = (f32[512,1024]{1,0:T(8,128)}, f32[512,1024]{1,0:T(8,128)S(1)}, u32[]{:S(2)}) copy-start(f32[512,1024]{1,0:T(8,128)S(1)} %get-tuple-element.296) | copy-start | bytes 6291460
  394.5 185.7 %copy-start.36 = (f32[512]{0:T(512)}, f32[512]{0:T(512)S(1)}, u32[]{:S(2)}) copy-start(f32[512]{0:T(512)S(1)} %broadcast_multiply_fusion.4) | copy-start | bytes 6148
  394.9 185.3 %copy-start.38 = (f32[512]{0:T(512)}, f32[512]{0:T(512)S(1)}, u32[]{:S(2)}) copy-start(f32[512]{0:T(512)S(1)} %add_rsqrt_fusion) | copy-start | bytes 6148
  452.9 88.6 %copy-start.27 = (bf16[2,256,1024]{2,1,0:T(8,128)(2,1)S(1)}, bf16[2,256,1024]{2,1,0:T(8,128)(2,1)}, u32[]{:S(2)}) copy-start(bf16[2,256,1024]{2,1,0:T(8,128)(2,1)} %param.22) | copy-start | bytes 3145732
  586.4 28.9 %all-to-all-start.2 = ((bf16[2,16,64,256]{3,2,0,1:T(8,128)(2,1)}), bf16[2,16,64,256]{3,2,0,1:T(8,128)(2,1)S(1)}, u32[]{:S(2)}, u32[]{:S(2)}) async-start(bf16[2,16,64,256]{3,2,0,1:T(8,128)(2,1)} %copy.179), calls=%async_computation.2 | async-start | bytes 2097152 | tf_op jit(solution)/shard_map/all_to_all | solution.py:201
  589.9 281.6 %all-reduce.9.cloned.1.call-start = ((), (), s32[]{:S(2)}) async-start(), calls=%async_computation.30 | async-start | bytes 16777216
  834.4 257.3 %reduce-scatter.25.cloned.1.call-start = ((), (), s32[]{:S(2)}) async-start(), calls=%async_computation.21 | async-start | bytes 4456448 | tf_op jit(solution)/shard_map/reduce_scatter | solution.py:229
  900.1 126.8 %all-to-all-start.3 = ((bf16[4,2,196608]{2,1,0:T(2,128)(2,1)}), bf16[4,2,196608]{2,1,0:T(2,128)(2,1)S(1)}, u32[]{:S(2)}, u32[]{:S(2)}) async-start(bf16[4,2,196608]{2,1,0:T(2,128)(2,1)} %reshape.282), calls=%async_computation.3 | async-start | bytes 6291456 | tf_op jit(solution)/shard_map/all_to_all | solution.py:217
  905.2 232.8 %reduce-scatter.37.cloned.1.call-start = ((), (), s32[]{:S(2)}) async-start(), calls=%async_computation.28 | async-start | bytes 557056
  1062.0 265.2 %reduce-scatter.33.cloned.1.call-start = ((), (), s32[]{:S(2)}) async-start(), calls=%async_computation.26 | async-start | bytes 11698176
  1083.4 452.9 %reduce-scatter.21.cloned.1.call-start = ((), (), s32[]{:S(2)}) async-start(), calls=%async_computation.19 | async-start | bytes 13369344 | tf_op jit(solution)/shard_map/reduce_scatter | solution.py:228
  1091.6 454.5 %reduce-scatter.27.cloned.1.call-start = ((), (), s32[]{:S(2)}) async-start(), calls=%async_computation.22 | async-start | bytes 196608 | tf_op jit(solution)/shard_map/reduce_scatter | solution.py:238
  1093.5 900.5 %reduce-scatter.29.cloned.1.call-start = ((), (), s32[]{:S(2)}) async-start(), calls=%async_computation.23 | async-start | bytes 22839296 | tf_op jit(solution)/shard_map/reduce_scatter | solution.py:230
  1106.9 896.9 %reduce-scatter.39.cloned.1.call-start = ((), (), s32[]{:S(2)}) async-start(), calls=%async_computation.29 | async-start | bytes 24576
  1139.5 876.4 %reduce-scatter.35.cloned.1.call-start = ((), (), s32[]{:S(2)}) async-start(), calls=%async_computation.27 | async-start | bytes 1007616
  1329.4 698.1 %reduce-scatter.23.cloned.1.call-start = ((), (), s32[]{:S(2)}) async-start(), calls=%async_computation.20 | async-start | bytes 589824 | tf_op jit(solution)/shard_map/reduce_scatter | solution.py:235
  1538.2 501.5 %reduce-scatter.31.cloned.1.call-start = ((), (), s32[]{:S(2)}) async-start(), calls=%async_computation.25 | async-start | bytes 2015232
  1546.1 452.6 %copy-start.8 = (bf16[2,256,1024]{2,1,0:T(8,128)(2,1)S(1)}, bf16[2,256,1024]{2,1,0:T(8,128)(2,1)}, u32[]{:S(2)}) copy-start(bf16[2,256,1024]{2,1,0:T(8,128)(2,1)} %param.21) | copy-start | bytes 3145732
  1546.1 452.6 %copy-start.13 = (f32[512,1024]{1,0:T(8,128)S(1)}, f32[512,1024]{1,0:T(8,128)}, u32[]{:S(2)}) copy-start(f32[512,1024]{1,0:T(8,128)} %get-tuple-element.259) | copy-start | bytes 6291460
  2002.4 38.8 %copy-start.31 = (f32[64,2624]{1,0:T(8,128)S(1)}, f32[64,2624]{1,0:T(8,128)}, u32[]{:S(2)}) copy-start(f32[64,2624]{1,0:T(8,128)} %param.32) | copy-start | bytes 2015236
  (44 other events, 395.8 us)
Sparse Core Ops, SparseCore 0:
  10.9 96.9 all-gather.11
  208.1 8.8 all-gather.21
  219.2 11.7 all-gather.13
  233.6 61.9 all-gather.15
  298.7 154.1 all-gather.17
  456.1 85.3 all-gather.19
  834.5 37.0 all-reduce.8
  873.8 165.9 reduce-scatter.24
  1062.1 75.8 reduce-scatter.36
  1144.5 182.5 reduce-scatter.32
  1332.9 203.3 reduce-scatter.20
  1539.0 7.0 reduce-scatter.26
  1548.5 445.4 reduce-scatter.28
  1996.7 7.0 reduce-scatter.38
  2006.6 9.2 reduce-scatter.34
  2018.6 8.9 reduce-scatter.22
  2029.7 9.9 reduce-scatter.30
where the time goes:
time: 2060 us; the launch traced here: 2050 us
  waiting for transfers between devices  1270 us (62%)
  matrix products  316 us (15%)
  blocking collectives  183 us (9%)
  other arithmetic  130 us (6%)
  local copies, waits for them, and re-layouts  129 us (6%)
    reduce_scatter x1, waiting for transfers between devices, on_device(): lax.psum_scatter(grad_in, ('dp', 'seq'), scatter_dimension=0, tiled=True)  444 us
    unnamed x23, waiting for transfers between devices  270 us
    reduce_scatter x1, waiting for transfers between devices, on_device(): lax.psum_scatter(grad_qkv, ('dp', 'seq'), scatter_dimension=0, tiled=True)  207 us
    all_to_all x1, waiting for transfers between devices, on_device(): lax.all_to_all(qkv_heads_grad, 'seq', split_axis=4, concat_axis=2, tiled=...  122 us
    all_gather x1, waiting for transfers between devices, on_device(): lax.all_gather(cols_ffn, ('dp', 'seq'), axis=0, tiled=True)  75.8 us
    all_to_all x1, blocking collectives, on_device(): lax.all_to_all(proj_qkv, 'seq', split_axis=2, concat_axis=4, tiled=True)  73.5 us
    all_gather x1, waiting for transfers between devices, on_device(): lax.all_gather(cols_in, ('dp', 'seq'), axis=0, tiled=True)  58 us
    all_to_all x1, blocking collectives, on_device(): lax.all_to_all(head_out, 'seq', split_axis=3, concat_axis=1, tiled=True)  56.7 us
  transfers between devices with their start and end apart: 19, of which 15 were waited for; matrix products, arithmetic and copies ran while one was open for 13% of the time, Pallas kernels for 0%

commit v1 on v0

v1 whole, which is shorter than its diff:
```python
import jax
import jax.numpy as jnp
from jax import lax
from jax.experimental import pallas as pl
from jax.experimental.pallas import tpu as pltpu
from jax.sharding import PartitionSpec as P

D = 1024
H = 16
HD = 64
FF = 2624
STEP = 10
OUT_FAN = 1


EPS_NORM = 1e-05
ROPE_BASE = 160000.0
BETA_ONE = 0.9
BETA_TWO = 0.999
ADAM_EPS = 1e-08
WEIGHT_DECAY = 0.01
LR_FACTOR = 3.0
LR_GAIN = 1.0


def rotate(rows, cos_part, sin_part):
    half = HD // 2
    low_half = rows[:half]
    high_half = rows[half:]
    return jnp.concatenate(
        [
            low_half * cos_part - high_half * sin_part,
            high_half * cos_part + low_half * sin_part,
        ],
        axis=0,
    )


def mm(left, right):
    return jnp.dot(left, right, preferred_element_type=jnp.float32)


def attend_kernel(qkv_ref, cos_ref, sin_ref, out_ref, lse_ref, q_s, k_s, v_s):
    parts, _, _, _, cols = qkv_ref.shape
    for z in range(parts):
        at = slice(z * cols, (z + 1) * cols)
        cos_part, sin_part = cos_ref[z], sin_ref[z]
        q_rot = rotate(qkv_ref[z, 0, 0].astype(jnp.float32), cos_part, sin_part)
        q_s[z] = (q_rot.astype(jnp.bfloat16).astype(jnp.float32) * HD ** (-0.5)).astype(jnp.bfloat16)
        k_rot = rotate(qkv_ref[z, 0, 1].astype(jnp.float32), cos_part, sin_part)
        k_s[at, :] = k_rot.T.astype(jnp.bfloat16)
        v_s[:, at] = qkv_ref[z, 0, 2]

    def block(z, carry):
        scores = mm(k_s[...], q_s[z])
        top = jnp.max(scores, axis=0, keepdims=True)
        exp_scores = jnp.exp(scores - top)
        total = jnp.sum(exp_scores, axis=0, keepdims=True)
        out = mm(v_s[...], exp_scores.astype(jnp.bfloat16))
        out_ref[z, 0] = (out / total).astype(jnp.bfloat16)
        lse_ref[z, 0] = top + jnp.log(total)
        return carry

    lax.fori_loop(0, parts, block, 0)


def attend_back_kernel(
    qkv_ref, cos_ref, sin_ref, out_ref, lse_ref, grad_ref, res_ref,
    q_s, q_rows, k_s, k_cols, v_rows, g_rows, dk, dv,
):
    parts, _, _, _, cols = qkv_ref.shape
    for z in range(parts):
        at = slice(z * cols, (z + 1) * cols)
        cos_part, sin_part = cos_ref[z], sin_ref[z]
        q_rot = rotate(qkv_ref[z, 0, 0].astype(jnp.float32), cos_part, sin_part)
        q_rot = q_rot.astype(jnp.bfloat16).astype(jnp.float32) * HD ** (-0.5)
        q_s[z] = q_rot.astype(jnp.bfloat16)
        q_rows[z] = q_rot.T.astype(jnp.bfloat16)
        k_rot = rotate(qkv_ref[z, 0, 1].astype(jnp.float32), cos_part, sin_part)
        k_cols[:, at] = k_rot.astype(jnp.bfloat16)
        k_s[at, :] = k_rot.T.astype(jnp.bfloat16)
        v_rows[at, :] = qkv_ref[z, 0, 2].astype(jnp.float32).T.astype(jnp.bfloat16)
        g_rows[z] = grad_ref[z, 0].astype(jnp.float32).T.astype(jnp.bfloat16)
    dk[...] = jnp.zeros_like(dk)
    dv[...] = jnp.zeros_like(dv)

    def block(z, carry):
        grad = grad_ref[z, 0]
        inner = jnp.sum(
            grad.astype(jnp.float32) * out_ref[z, 0].astype(jnp.float32), axis=0, keepdims=True
        )
        probs = jnp.exp(mm(k_s[...], q_s[z]) - lse_ref[z, 0])
        dv[...] += mm(probs.astype(jnp.bfloat16), g_rows[z])
        score_grad = (probs * (mm(v_rows[...], grad) - inner)).astype(jnp.bfloat16)
        dk[...] += mm(score_grad, q_rows[z])
        dq = mm(k_cols[...], score_grad) * HD ** (-0.5)
        res_ref[z, 0, 0] = rotate(dq, cos_ref[z], -sin_ref[z]).astype(jnp.bfloat16)
        return carry

    lax.fori_loop(0, parts, block, 0)
    for z in range(parts):
        at = slice(z * cols, (z + 1) * cols)
        dk_cols = dk[at, :].T
        res_ref[z, 0, 1] = rotate(dk_cols, cos_ref[z], -sin_ref[z]).astype(jnp.bfloat16)
        res_ref[z, 0, 2] = dv[at, :].T.astype(jnp.bfloat16)


def pair_spec(parts, *rest):
    zeros = (0,) * len(rest)
    return pl.BlockSpec((parts, 1) + rest, lambda pair: (0, pair) + zeros)


def attend(qkv, cos_tab, sin_tab):
    parts, pairs, _, _, cols = qkv.shape
    length = parts * cols
    table = pl.BlockSpec(cos_tab.shape, lambda pair: (0, 0, 0))
    return pl.pallas_call(
        attend_kernel,
        grid=(pairs,),
        in_specs=[pair_spec(parts, 3, HD, cols), table, table],
        out_specs=[pair_spec(parts, HD, cols), pair_spec(parts, 1, cols)],
        out_shape=[
            jax.ShapeDtypeStruct((parts, pairs, HD, cols), jnp.bfloat16),
            jax.ShapeDtypeStruct((parts, pairs, 1, cols), jnp.float32),
        ],
        scratch_shapes=[
            pltpu.VMEM((parts, HD, cols), jnp.bfloat16),
            pltpu.VMEM((length, HD), jnp.bfloat16),
            pltpu.VMEM((HD, length), jnp.bfloat16),
        ],
        compiler_params=pltpu.CompilerParams(vmem_limit_bytes=40 * 2**20),
        cost_estimate=pl.CostEstimate(
            flops=16 * pairs * length * length * HD,
            bytes_accessed=8 * pairs * length * HD,
            transcendentals=pairs * length * length,
        ),
        name="attend",
    )(qkv, cos_tab, sin_tab)


def attend_back(qkv, cos_tab, sin_tab, out, lse, grad):
    parts, pairs, _, _, cols = qkv.shape
    length = parts * cols
    table = pl.BlockSpec(cos_tab.shape, lambda pair: (0, 0, 0))
    return pl.pallas_call(
        attend_back_kernel,
        grid=(pairs,),
        in_specs=[
            pair_spec(parts, 3, HD, cols),
            table,
            table,
            pair_spec(parts, HD, cols),
            pair_spec(parts, 1, cols),
            pair_spec(parts, HD, cols),
        ],
        out_specs=pair_spec(parts, 3, HD, cols),
        out_shape=jax.ShapeDtypeStruct(qkv.shape, jnp.bfloat16),
        scratch_shapes=[
            pltpu.VMEM((parts, HD, cols), jnp.bfloat16),
            pltpu.VMEM((parts, cols, HD), jnp.bfloat16),
            pltpu.VMEM((length, HD), jnp.bfloat16),
            pltpu.VMEM((HD, length), jnp.bfloat16),
            pltpu.VMEM((length, HD), jnp.bfloat16),
            pltpu.VMEM((parts, cols, HD), jnp.bfloat16),
            pltpu.VMEM((length, HD), jnp.float32),
            pltpu.VMEM((length, HD), jnp.float32),
        ],
        compiler_params=pltpu.CompilerParams(vmem_limit_bytes=48 * 2**20),
        cost_estimate=pl.CostEstimate(
            flops=40 * pairs * length * length * HD,
            bytes_accessed=20 * pairs * length * HD,
            transcendentals=pairs * length * length,
        ),
        name="attend_back",
    )(qkv, cos_tab, sin_tab, out, lse, grad)


def swap(values):
    return lax.ppermute(values, "qblk", [(0, 1), (1, 0)])


def norm_fwd(values, gain_row):
    row_mean = jnp.mean(values, axis=-1, keepdims=True)
    centered = values - row_mean
    row_var = jnp.mean(centered * centered, axis=-1, keepdims=True)
    inv_std = lax.rsqrt(row_var + EPS_NORM)
    normed = centered * inv_std
    return (normed, inv_std, (normed * gain_row).astype(jnp.bfloat16))


def norm_back(upstream, normed, inv_std, gain_row):
    scaled = upstream * gain_row
    return inv_std * (
        scaled
        - jnp.mean(scaled, axis=-1, keepdims=True)
        - normed * jnp.mean(scaled * normed, axis=-1, keepdims=True)
    )


def gated(gate_part, up_part):
    return jax.nn.gelu(gate_part, approximate=False) * up_part


def adam_step(weight, grad_sum, moment, second, learn_rate, weight_decay):
    moment_new = BETA_ONE * moment + (1.0 - BETA_ONE) * grad_sum
    second_new = BETA_TWO * second + (1.0 - BETA_TWO) * grad_sum * grad_sum
    update = (
        moment_new
        / (1.0 - BETA_ONE**STEP)
        / (jnp.sqrt(second_new / (1.0 - BETA_TWO**STEP)) + ADAM_EPS)
    )
    return (moment_new, second_new, weight - learn_rate * (update + weight_decay * weight))


def on_device(
    tokens,
    cotangent,
    w_qkv,
    w_out,
    w_in,
    w_ffn,
    gains,
    first_qkv,
    second_qkv,
    first_out,
    second_out,
    first_in,
    second_in,
    first_ffn,
    second_ffn,
    first_gain,
    second_gain,
):
    n_seq = lax.axis_size("seq")
    core = lax.axis_index("qblk")
    first = core == 0
    seq_count, tok_local, width = tokens.shape
    row_count = seq_count * tok_local
    chip_tok = 2 * tok_local
    heads = H // 2
    pairs = heads * seq_count // n_seq
    both = ("dp", "seq")

    def ordered(own, other, axis):
        return jnp.where(
            first,
            jnp.concatenate([own, other], axis=axis),
            jnp.concatenate([other, own], axis=axis),
        )

    def gather(shard):
        return lax.all_gather(shard, both, axis=0, tiled=True)

    def scatter(grad):
        return lax.psum_scatter(grad, both, scatter_dimension=0, tiled=True)

    def with_other(rows):
        return jnp.concatenate([rows, swap(rows)], axis=0)

    def sum_own(part):
        other = swap(part[row_count:].astype(jnp.bfloat16))
        return part[:row_count] + other.astype(jnp.float32)

    third = w_qkv.shape[1] // 3
    low_qkv = w_qkv.astype(jnp.bfloat16)
    col_a, col_b, col_c = low_qkv[:, :third], low_qkv[:, third : 2 * third], low_qkv[:, 2 * third :]
    col_r = swap(col_b)
    full_gain = lax.all_gather(
        gains.astype(jnp.bfloat16), ("dp", "seq", "qblk"), axis=1, tiled=True
    )
    full_qkv = gather(
        jnp.where(
            first,
            jnp.concatenate([col_a, col_c, col_r], axis=1),
            jnp.concatenate([col_r, col_a, col_c], axis=1),
        )
    )
    low_out = w_out.astype(jnp.bfloat16)
    shard_out = ordered(low_out, swap(low_out), 1)
    low_in = w_in.astype(jnp.bfloat16)
    part = low_in.shape[1] // 2
    in_r = swap(jnp.where(first, low_in[:, part:], low_in[:, :part]))
    shard_gate = jnp.where(first, low_in[:, :part], in_r)
    shard_up = jnp.where(first, in_r, low_in[:, part:])
    low_ffn = w_ffn.astype(jnp.bfloat16)
    full_qkv, shard_out, shard_gate, shard_up, low_ffn = lax.optimization_barrier(
        (full_qkv, shard_out, shard_gate, shard_up, low_ffn)
    )
    full_out = gather(shard_out)
    full_gate = gather(shard_gate)
    full_up = gather(shard_up)
    full_ffn = gather(low_ffn)

    place_ids = jnp.arange(n_seq * chip_tok, dtype=jnp.int32).reshape(n_seq, 1, chip_tok)
    in_chip = place_ids % chip_tok
    positions = (
        place_ids - in_chip + (in_chip // tok_local + core) % 2 * tok_local + in_chip % tok_local
    ).astype(jnp.float32)
    half_dim = HD // 2
    inv_freq = ROPE_BASE ** (-2.0 * jnp.arange(half_dim, dtype=jnp.float32) / HD)
    angles = inv_freq[None, :, None] * positions
    cos_tab, sin_tab = jnp.cos(angles), jnp.sin(angles)

    def to_heads(cols, kinds):
        split = cols.reshape(kinds, heads, HD, 2, seq_count, tok_local)
        split = split.transpose(1, 4, 0, 2, 3, 5).reshape(n_seq, pairs, kinds, HD, chip_tok)
        return lax.all_to_all(split, "seq", split_axis=0, concat_axis=0, tiled=True)

    def from_heads(moved, kinds):
        back = lax.all_to_all(moved, "seq", split_axis=0, concat_axis=0, tiled=True)
        back = back.reshape(heads, seq_count, kinds, HD, 2, tok_local)
        return back.transpose(2, 0, 3, 4, 1, 5).reshape(kinds * heads * HD, 2 * row_count)

    gain_rows = full_gain.astype(jnp.float32)
    resid_in = tokens.astype(jnp.float32).reshape(row_count, width)
    normed_one, inv_one, attn_own = norm_fwd(resid_in, gain_rows[0])
    attn_in = with_other(attn_own)
    grad_own = cotangent.reshape(row_count, width).astype(jnp.bfloat16)
    grad_low = with_other(grad_own)
    proj = jnp.einsum("dn,td->nt", full_qkv, attn_in, preferred_element_type=jnp.float32)
    qkv = to_heads(proj.astype(jnp.bfloat16), 3)
    head_out, lse = attend(qkv, cos_tab, sin_tab)
    attn_cols = from_heads(head_out[:, :, None], 1)
    attn = ordered(attn_cols[:, :row_count], swap(attn_cols[:, row_count:]), 0)
    resid_mid = resid_in + jnp.einsum(
        "ft,fd->td", attn, full_out, preferred_element_type=jnp.float32
    )
    normed_two, inv_two, ffn_own = norm_fwd(resid_mid, gain_rows[1])
    ffn_in = with_other(ffn_own)
    gate_part = mm(ffn_in, full_gate)
    up_part = mm(ffn_in, full_up)
    hidden = gated(gate_part, up_part).astype(jnp.bfloat16)
    hidden_grad = mm(grad_low, full_ffn)
    gate_grad, up_grad = jax.vjp(gated, gate_part, up_part)[1](hidden_grad)
    gate_grad = gate_grad.astype(jnp.bfloat16)
    up_grad = up_grad.astype(jnp.bfloat16)

    def outer(left, right):
        return jnp.einsum("ta,tb->ab", left, right, preferred_element_type=jnp.float32).astype(
            jnp.bfloat16
        )

    def times_t(left, right):
        return jnp.einsum("tf,df->td", left, right, preferred_element_type=jnp.float32)

    ffn_in_grad = sum_own(times_t(gate_grad, full_gate) + times_t(up_grad, full_up))
    gain_two_grad = jnp.sum(ffn_in_grad * normed_two, axis=0)
    grad_y = cotangent.astype(jnp.float32).reshape(row_count, width)
    mid_grad = grad_y + norm_back(ffn_in_grad, normed_two, inv_two, gain_rows[1])
    mid_low = mid_grad.astype(jnp.bfloat16)
    grad_gate = outer(ffn_in, gate_grad)
    grad_up = outer(ffn_in, up_grad)
    grad_ffn = outer(grad_low, hidden)
    attn_grad = jnp.einsum("fd,td->ft", full_out, mid_low, preferred_element_type=jnp.float32)
    attn_grad = attn_grad.astype(jnp.bfloat16)
    span = heads * HD
    mine = lax.dynamic_slice_in_dim(attn_grad, core * span, span, axis=0)
    theirs = lax.dynamic_slice_in_dim(attn_grad, (1 - core) * span, span, axis=0)
    heads_grad = to_heads(jnp.concatenate([mine, swap(theirs)], axis=1), 1)
    heads_grad, grad_gate, grad_up, grad_ffn = lax.optimization_barrier(
        (heads_grad, grad_gate, grad_up, grad_ffn)
    )
    sum_gate = scatter(grad_gate)
    sum_up = scatter(grad_up)
    sum_ffn = scatter(grad_ffn).astype(jnp.float32)
    grad_out = jnp.einsum("ft,td->fd", attn, mid_low, preferred_element_type=jnp.float32)
    out_cols = w_out.shape[1]
    out_mine = lax.dynamic_slice_in_dim(grad_out, core * out_cols, out_cols, axis=1)
    out_theirs = lax.dynamic_slice_in_dim(grad_out, (1 - core) * out_cols, out_cols, axis=1)
    out_sum = out_mine + swap(out_theirs.astype(jnp.bfloat16)).astype(jnp.float32)
    sum_out = scatter(out_sum.astype(jnp.bfloat16)).astype(jnp.float32)
    block_part = times_t(hidden, full_ffn)
    block_out = (resid_mid + sum_own(block_part)).astype(jnp.bfloat16).reshape(tokens.shape)

    res = attend_back(qkv, cos_tab, sin_tab, head_out, lse, heads_grad[:, :, 0])
    qkv_grad = from_heads(res, 3)
    grad_qkv = jnp.einsum("td,nt->dn", attn_in, qkv_grad, preferred_element_type=jnp.float32)
    rows_qkv = scatter(grad_qkv.astype(jnp.bfloat16))
    in_grad = sum_own(
        jnp.einsum("nt,dn->td", qkv_grad, full_qkv, preferred_element_type=jnp.float32)
    )
    gain_one_grad = jnp.sum(in_grad * normed_one, axis=0)
    grad_x = mid_grad + norm_back(in_grad, normed_one, inv_one, gain_rows[0])
    sum_gain = lax.psum_scatter(
        jnp.stack([gain_one_grad, gain_two_grad]),
        ("dp", "seq", "qblk"),
        scatter_dimension=1,
        tiled=True,
    )
    q_sum, k_sum, v_sum = rows_qkv[:, :third], rows_qkv[:, third : 2 * third], rows_qkv[:, 2 * third :]
    qkv_r = swap(jnp.where(first, v_sum, q_sum))
    sum_qkv = jnp.concatenate(
        [jnp.where(first, q_sum, k_sum), qkv_r, jnp.where(first, k_sum, v_sum)], axis=1
    ).astype(jnp.float32)
    gate_up_r = swap(jnp.where(first, sum_up, sum_gate))
    sum_in = ordered(jnp.where(first, sum_gate, sum_up), gate_up_r, 1).astype(jnp.float32)
    new_qkv = adam_step(
        w_qkv, sum_qkv, first_qkv, second_qkv, LR_FACTOR * D ** (-0.5), WEIGHT_DECAY
    )
    new_out = adam_step(
        w_out, sum_out, first_out, second_out, LR_FACTOR * OUT_FAN ** (-0.5), WEIGHT_DECAY
    )
    new_in = adam_step(w_in, sum_in, first_in, second_in, LR_FACTOR * D ** (-0.5), WEIGHT_DECAY)
    new_ffn = adam_step(
        w_ffn, sum_ffn, first_ffn, second_ffn, LR_FACTOR * FF ** (-0.5), WEIGHT_DECAY
    )
    new_gain = adam_step(gains, sum_gain, first_gain, second_gain, LR_GAIN, 0.0)
    return (
        block_out,
        grad_x.reshape(tokens.shape),
        new_qkv[0],
        new_qkv[1],
        new_qkv[2],
        new_out[0],
        new_out[1],
        new_out[2],
        new_in[0],
        new_in[1],
        new_in[2],
        new_ffn[0],
        new_ffn[1],
        new_ffn[2],
        new_gain[0],
        new_gain[1],
        new_gain[2],
    )


def solution(mesh):
    placed = (
        P("dp", ("seq", "qblk"), None),
        P("dp", ("seq", "qblk"), None),
        P(("dp", "seq"), "qblk"),
        P(("dp", "seq"), "qblk"),
        P(("dp", "seq"), "qblk"),
        P(("dp", "seq"), "qblk"),
        P(None, ("dp", "seq", "qblk")),
        P(("dp", "seq"), "qblk"),
        P(("dp", "seq"), "qblk"),
        P(("dp", "seq"), "qblk"),
        P(("dp", "seq"), "qblk"),
        P(("dp", "seq"), "qblk"),
        P(("dp", "seq"), "qblk"),
        P(("dp", "seq"), "qblk"),
        P(("dp", "seq"), "qblk"),
        P(None, ("dp", "seq", "qblk")),
        P(None, ("dp", "seq", "qblk")),
    )
    return jax.shard_map(
        on_device,
        mesh=mesh,
        in_specs=placed,
        out_specs=(
            P("dp", ("seq", "qblk"), None),
            P("dp", ("seq", "qblk"), None),
            P(("dp", "seq"), "qblk"),
            P(("dp", "seq"), "qblk"),
            P(("dp", "seq"), "qblk"),
            P(("dp", "seq"), "qblk"),
            P(("dp", "seq"), "qblk"),
            P(("dp", "seq"), "qblk"),
            P(("dp", "seq"), "qblk"),
            P(("dp", "seq"), "qblk"),
            P(("dp", "seq"), "qblk"),
            P(("dp", "seq"), "qblk"),
            P(("dp", "seq"), "qblk"),
            P(("dp", "seq"), "qblk"),
            P(None, ("dp", "seq", "qblk")),
            P(None, ("dp", "seq", "qblk")),
            P(None, ("dp", "seq", "qblk")),
        ),
        check_vma=False,
    )
```

time: 2060 us -> 1150 us (0.56)
  waiting for transfers between devices: 1270 us -> 778 us
  matrix products: 316 us -> 94.1 us
  blocking collectives: 183 us -> 38.9 us
  Pallas kernels: 0 us -> 85.7 us
  other arithmetic: 130 us -> 50.8 us
  local copies, waits for them, and re-layouts: 129 us -> 66.2 us
    reduce_scatter x5, waiting for transfers between devices: 659 us -> 276 us  [scatter(): return lax.psum_scatter(grad, both, scatter_dimension=0, tiled=True)]
    dot_general x26 -> x15, matrix products: 316 us -> 94.1 us  [the longest x3 34.5 us: mm(): return jnp.dot(left, right, preferred_element_type=jnp.float32)]
    unnamed x23 -> x12, waiting for transfers between devices: 270 us -> 125 us
    all_to_all x2 -> x0, blocking collectives: 130 us -> none  [the longest x1 73.5 us: on_device(): lax.all_to_all(proj_qkv, 'seq', split_axis=2, concat_axis=4, tiled=True)]
    all_to_all x2 -> x4, waiting for transfers between devices: 147 us -> 239 us  [the longest x2 143 us: from_heads(): back = lax.all_to_all(moved, 'seq', split_axis=0, concat_axis=0, tiled=True)]
    pallas_call x0 -> x2, Pallas kernels: none -> 85.7 us  [the longest x1 50.1 us: attend_back(): pl.pallas_call(attend_back_kernel, grid=(pairs,), in_specs=[pair_spec(par...]
    all_gather x6 -> x5, waiting for transfers between devices: 189 us -> 127 us  [gather(): return lax.all_gather(shard, both, axis=0, tiled=True)]
    convert_element_type x11 -> x9, other arithmetic: 70 us -> 19.8 us  [the longest x1 12.9 us: on_device(): gate_grad = gate_grad.astype(jnp.bfloat16)]
  transfers between devices with their start and end apart: 19 -> 29, of which waited for: 15 -> 16; matrix products, arithmetic and copies ran while one was open for 13% -> 13% of each run, Pallas kernels for 0% -> 7%
where the time goes in v1:
time: 1150 us
  waiting for transfers between devices  778 us (68%)
  matrix products  94.1 us (8%)
  Pallas kernels  85.7 us (7%)
  local copies, waits for them, and re-layouts  66.2 us (6%)
  other arithmetic  50.8 us (4%)
  blocking collectives  38.9 us (3%)
  starting transfers between devices  18.5 us (2%)
  between operations  14.8 us (1%)
    reduce_scatter x5, waiting for transfers between devices, scatter(): return lax.psum_scatter(grad, both, scatter_dimension=0, tiled=True)  276 us
    all_to_all x2, waiting for transfers between devices, from_heads(): back = lax.all_to_all(moved, 'seq', split_axis=0, concat_axis=0, tiled=True)  143 us
    all_gather x5, waiting for transfers between devices, gather(): return lax.all_gather(shard, both, axis=0, tiled=True)  127 us
    unnamed x12, waiting for transfers between devices  125 us
    all_to_all x2, waiting for transfers between devices, to_heads(): return lax.all_to_all(split, 'seq', split_axis=0, concat_axis=0, tiled=True)  96.6 us
    pallas_call x1, Pallas kernels, attend_back(): pl.pallas_call(attend_back_kernel, grid=(pairs,), in_specs=[pair_spec(par...  50.1 us
    all_gather x1, blocking collectives, on_device(): lax.all_gather(gains.astype(jnp.bfloat16), ('dp', 'seq', 'qblk'), axis=1,...  38.9 us
    pallas_call x1, Pallas kernels, attend(): pl.pallas_call(attend_kernel, grid=(pairs,), in_specs=[pair_spec(parts, 3...  35.6 us
  transfers between devices with their start and end apart: 29, of which 16 were waited for; matrix products, arithmetic and copies ran while one was open for 13% of the time, Pallas kernels for 7%

profile of v1, /device:TPU:0, one launch (start us, length us, event | category | flops | bytes accessed | tf_op | source)
XLA Modules:
  0.0 1146.8 jit_solution(11073059327450353530)
XLA Ops:
  15.6 66.6 %all-gather.7.cloned.1.call-done = bf16[1024,1536]{1,0:T(8,128)(2,1)} async-done(((bf16[64,1536]{1,0:T(8,128)(2,1)}), bf16[1024,1536]{1,0:T(8,128)(2,1)}) %all-gather.7.cloned.1.call-update) | async-done | bytes 3145744 | tf_op jit(solution)/shard_map/all_gather | solution.py:252
  82.3 38.9 %all-gather = bf16[32,32,2]{1,2,0:T(2,128)(2,1)S(1)} all-gather(bf16[1,32,2]{1,2,0:T(2,128)(2,1)S(1)} %convert_bitcast_fusion), channel_id=1, replica_groups=mesh['dp'=4,'seq'=4,'qblk'=2] {'dp','seq','qblk'}, dimensions={0}, use_global_device_ids=true | all-gather | bytes 4224 | tf_op jit(solution)/shard_map/all_gather | solution.py:268
  126.2 5.9 convolution_convert_fusion.4
  132.1 4.8 reshape.262
  136.9 4.9 copy.136
  141.8 6.0 reshape.263
  153.9 80.6 %all-to-all-done.qkv_ref = bf16[4,4,3,64,512]{4,3,2,1,0:T(8,128)(2,1)S(1)} async-done(((bf16[4,4,3,64,512]{4,3,2,1,0:T(8,128)(2,1)}), bf16[4,4,3,64,512]{4,3,2,1,0:T(8,128)(2,1)S(1)}, u32[]{:S(2)}, u32[]{:S(2)}) %all-to-all-start) | async-done | bytes 3145760 | tf_op jit(solution)/shard_map/all_to_all | solution.py:307
  235.6 35.6 %attend.1 = (bf16[4,4,64,512]{3,2,1,0:T(8,128)(2,1)S(1)}, f32[4,4,1,512]{3,2,1,0:T(1,128)S(1)}) custom-call(bf16[4,4,3,64,512]{4,3,2,1,0:T(8,128)(2,1)S(1)} %all-to-all-done.qkv_ref, f32[4,32,512]{2,1,0:T(8,128)S(1)} %copy-done.3, f32[4,32,512]{2,1,0:T(8,128)S(1)} %get-tuple-element.148.sin_ref), custom_call_target="tpu_custom_call" | custom-call | flops 17179869184 | bytes 4194304 | tf_op jit(solution)/shard_map/attend/pallas_call | solution.py:117
  276.7 33.9 %all-to-all-done.1 = bf16[4,4,1,64,512]{4,3,1,2,0:T(8,128)(2,1)S(1)} async-done(((bf16[4,4,1,64,512]{4,3,1,2,0:T(8,128)(2,1)}), bf16[4,4,1,64,512]{4,3,1,2,0:T(8,128)(2,1)S(1)}, u32[]{:S(2)}, u32[]{:S(2)}) %all-to-all-start.1) | async-done | bytes 1048608 | tf_op jit(solution)/shard_map/all_to_all | solution.py:310
  327.4 7.9 fusion.50
  335.3 7.8 fusion.49
  343.1 60.0 %all-gather.15.cloned.1.call-done = bf16[1024,1312]{1,0:T(8,128)(2,1)} async-done(((bf16[64,1312]{1,0:T(8,128)(2,1)}), bf16[1024,1312]{1,0:T(8,128)(2,1)}) %all-gather.15.cloned.1.call-update) | async-done | bytes 2686992 | tf_op jit(solution)/shard_map/all_gather | solution.py:252
  403.1 18.8 %multiply_convert_fusion = (bf16[1024,1312]{0,1:T(8,128)(2,1)}, f32[1024,1312]{0,1:T(8,128)S(1)}, f32[1024,1312]{0,1:T(8,128)S(1)}) fusion(f32[1024,1312]{0,1:T(8,128)} %fusion.50, bf16[1024,1312]{1,0:T(8,128)(2,1)} %all-gather.15.cloned.1.call-done, bf16[512,1024]{1,0:T(8,128)(2,1)} %collective-permute-done.7, bf16[512,1024]{1,0:T(8,128)(2,1)S(1)} %bitcast.101), kind=kOutput, calls=%fused_computation.2 | convolution fusion | flops 2844327936 | bytes 23592960 | tf_op jit(solution)/shard_map/dot_general | solution.py:40
  422.0 12.9 %add_convert_fusion = (bf16[1024,1312]{0,1:T(8,128)(2,1)}, bf16[1024,1312]{0,1:T(8,128)(2,1)}) fusion(f32[1024,1312]{0,1:T(8,128)S(1)} %get-tuple-element.129, f32[1024,1312]{0,1:T(8,128)S(1)} %get-tuple-element.156, f32[1024,1312]{0,1:T(8,128)S(1)} %copy-done.17, f32[1024,1312]{0,1:T(8,128)S(1)} %copy-done.16), kind=kLoop, calls=%fused_computation.3 | loop fusion | flops 24182784 | bytes 26869760 | tf_op jit(solution)/shard_map/convert_element_type | solution.py:335
  434.9 6.3 fusion.66
  477.3 7.0 convolution_convert_fusion.2
  484.3 6.0 convolution_convert_fusion.1
  490.3 5.5 convolution_convert_fusion
  495.8 16.0 %all-to-all-done.2 = bf16[4,4,1,64,512]{4,3,1,2,0:T(8,128)(2,1)S(1)} async-done(((bf16[4,4,1,64,512]{4,3,1,2,0:T(8,128)(2,1)}), bf16[4,4,1,64,512]{4,3,1,2,0:T(8,128)(2,1)S(1)}, u32[]{:S(2)}, u32[]{:S(2)}) %all-to-all-start.2) | async-done | bytes 1048608 | tf_op jit(solution)/shard_map/all_to_all | solution.py:307
  511.8 4.5 copy.123
  516.4 4.6 copy.121
  521.1 50.1 %attend_back.1 = bf16[4,4,3,64,512]{4,3,2,1,0:T(8,128)(2,1)} custom-call(bf16[4,4,3,64,512]{4,3,2,1,0:T(8,128)(2,1)} %copy-done, f32[4,32,512]{2,1,0:T(8,128)S(1)} %copy-done.4, f32[4,32,512]{2,1,0:T(8,128)S(1)} %get-tuple-element.148.sin_ref, bf16[4,4,64,512]{3,2,1,0:T(8,128)(2,1)S(1)} %copy-done.2, f32[4,4,1,512]{3,2,1,0:T(1,128)S(1)} %get-tuple-element.34.lse_ref, ...), custom_call_target="tpu_custom_call" | custom-call | flops 42949672960 | bytes 10485760 | tf_op jit(solution)/shard_map/attend_back/pallas_call | solution.py:145
  574.9 4.6 copy.125
  579.6 109.0 %all-to-all-done.3 = bf16[4,4,3,64,512]{4,3,2,1,0:T(8,128)(2,1)S(1)} async-done(((bf16[4,4,3,64,512]{4,3,2,1,0:T(8,128)(2,1)}), bf16[4,4,3,64,512]{4,3,2,1,0:T(8,128)(2,1)S(1)}, u32[]{:S(2)}, u32[]{:S(2)}) %all-to-all-start.3) | async-done | bytes 3145760 | tf_op jit(solution)/shard_map/all_to_all | solution.py:310
  691.8 6.8 copy.135
  698.6 3.9 reshape.275
  702.5 6.4 fusion.67
  714.0 7.1 convolution_convert_fusion.3
  723.8 58.7 %reduce-scatter.19.cloned.1.call-done = bf16[64,1312]{1,0:T(8,128)(2,1)} async-done(((bf16[1024,1312]{1,0:T(8,128)(2,1)}), bf16[64,1312]{1,0:T(8,128)(2,1)}) %reduce-scatter.19.cloned.1.call-update) | async-done | bytes 167952 | tf_op jit(solution)/shard_map/reduce_scatter | solution.py:255
  784.2 85.8 %reduce-scatter.23.cloned.1.call-done = bf16[64,1312]{1,0:T(8,128)(2,1)} async-done(((bf16[1024,1312]{1,0:T(8,128)(2,1)}), bf16[64,1312]{1,0:T(8,128)(2,1)}) %reduce-scatter.23.cloned.1.call-update) | async-done | bytes 167952 | tf_op jit(solution)/shard_map/reduce_scatter | solution.py:255
  879.4 124.2 %reduce-scatter.25.cloned.1.call-done = f32[32,2]{1,0:T(8,128)} async-done(((f32[1024,2]{1,0:T(8,128)}), f32[32,2]{1,0:T(8,128)}) %reduce-scatter.25.cloned.1.call-update) | async-done | bytes 272
  1004.4 131.1 %reduce-scatter.15.cloned.1.call-done = bf16[64,1536]{1,0:T(8,128)(2,1)} async-done(((bf16[1024,1536]{1,0:T(8,128)(2,1)}), bf16[64,1536]{1,0:T(8,128)(2,1)}) %reduce-scatter.15.cloned.1.call-update) | async-done | bytes 196624 | tf_op jit(solution)/shard_map/reduce_scatter | solution.py:255
  (226 shorter events, 109.9 us)
Async XLA Ops:
  7.2 75.0 %all-gather.7.cloned.1.call-start = ((), (), s32[]{:S(2)}) async-start(), calls=%async_computation.10 | async-start | bytes 3342336 | tf_op jit(solution)/shard_map/all_gather | solution.py:252
  8.4 1.4 collective-permute-start
  10.6 305.7 %all-gather.9.cloned.1.call-start = ((), (), s32[]{:S(2)}) async-start(), calls=%async_computation.11 | async-start | bytes 2228224 | tf_op jit(solution)/shard_map/all_gather | solution.py:252
  11.5 2.6 collective-permute-start.1
  13.2 1.6 collective-permute-start.2
  82.3 242.5 %all-gather.11.cloned.1.call-start = ((), (), s32[]{:S(2)}) async-start(), calls=%async_computation.12 | async-start | bytes 3063808 | tf_op jit(solution)/shard_map/all_gather | solution.py:252
  122.4 2.7 collective-permute-start.3
  147.8 86.7 %all-to-all-start = ((bf16[4,4,3,64,512]{4,3,2,1,0:T(8,128)(2,1)}), bf16[4,4,3,64,512]{4,3,2,1,0:T(8,128)(2,1)S(1)}, u32[]{:S(2)}, u32[]{:S(2)}) async-start(bf16[4,4,3,64,512]{4,3,2,1,0:T(8,128)(2,1)} %reshape.263), calls=%async_computation | async-start | bytes 6291456 | tf_op jit(solution)/shard_map/all_to_all | solution.py:307
  151.5 183.8 %all-gather.13.cloned.1.call-start = ((), (), s32[]{:S(2)}) async-start(), calls=%async_computation.13 | async-start | bytes 3063808 | tf_op jit(solution)/shard_map/all_gather | solution.py:252
  272.2 38.3 %all-to-all-start.1 = ((bf16[4,4,1,64,512]{4,3,1,2,0:T(8,128)(2,1)}), bf16[4,4,1,64,512]{4,3,1,2,0:T(8,128)(2,1)S(1)}, u32[]{:S(2)}, u32[]{:S(2)}) async-start(bf16[4,4,1,64,512]{4,3,1,2,0:T(8,128)(2,1)} %bitcast.92), calls=%async_computation.1 | async-start | bytes 2097152 | tf_op jit(solution)/shard_map/all_to_all | solution.py:310
  275.8 127.3 %all-gather.15.cloned.1.call-start = ((), (), s32[]{:S(2)}) async-start(), calls=%async_computation.14 | async-start | bytes 3063808 | tf_op jit(solution)/shard_map/all_gather | solution.py:252
  276.4 444.8 %reduce-scatter.17.cloned.1.call-start = ((), (), s32[]{:S(2)}) async-start(), calls=%async_computation.16 | async-start | bytes 1114112 | tf_op jit(solution)/shard_map/reduce_scatter | solution.py:255
  316.2 1.9 collective-permute-start.4
  324.2 3.2 collective-permute-start.5
  324.4 18.7 %collective-permute-start.7 = (bf16[512,1024]{1,0:T(8,128)(2,1)S(1)}, bf16[512,1024]{1,0:T(8,128)(2,1)}, u32[]{:S(2)}, u32[]{:S(2)}) collective-permute-start(bf16[512,1024]{1,0:T(8,128)(2,1)S(1)} %bitcast.100), channel_id=1, source_target_pairs={{0,1},{1,0},{2,3},{3,2},{4,5},{5,4},{6,7},{7,6},{8,9},{9,8},{10,11... | collective-permute-start | bytes 3145736 | tf_op jit(solution)/shard_map/ppermute | solution.py:179
  446.0 6.4 collective-permute-start.8
  451.9 3.1 collective-permute-start.6
  462.7 4.4 collective-permute-start.12
  466.5 2.2 collective-permute-start.9
  473.6 38.1 %all-to-all-start.2 = ((bf16[4,4,1,64,512]{4,3,1,2,0:T(8,128)(2,1)}), bf16[4,4,1,64,512]{4,3,1,2,0:T(8,128)(2,1)S(1)}, u32[]{:S(2)}, u32[]{:S(2)}) async-start(bf16[4,4,1,64,512]{4,3,1,2,0:T(8,128)(2,1)} %bitcast.13), calls=%async_computation.2 | async-start | bytes 2097152 | tf_op jit(solution)/shard_map/all_to_all | solution.py:307
  477.3 246.5 %reduce-scatter.21.cloned.1.call-start = ((), (), s32[]{:S(2)}) async-start(), calls=%async_computation.18 | async-start | bytes 3063808 | tf_op jit(solution)/shard_map/reduce_scatter | solution.py:255
  516.3 266.1 %reduce-scatter.19.cloned.1.call-start = ((), (), s32[]{:S(2)}) async-start(), calls=%async_computation.17 | async-start | bytes 3063808 | tf_op jit(solution)/shard_map/reduce_scatter | solution.py:255
  571.2 117.4 %all-to-all-start.3 = ((bf16[4,4,3,64,512]{4,3,2,1,0:T(8,128)(2,1)}), bf16[4,4,3,64,512]{4,3,2,1,0:T(8,128)(2,1)S(1)}, u32[]{:S(2)}, u32[]{:S(2)}) async-start(bf16[4,4,3,64,512]{4,3,2,1,0:T(8,128)(2,1)} %attend_back.1), calls=%async_computation.3 | async-start | bytes 6291456 | tf_op jit(solution)/shard_map/all_to_all | solution.py:310
  574.9 295.1 %reduce-scatter.23.cloned.1.call-start = ((), (), s32[]{:S(2)}) async-start(), calls=%async_computation.19 | async-start | bytes 3063808 | tf_op jit(solution)/shard_map/reduce_scatter | solution.py:255
  579.6 424.0 %reduce-scatter.25.cloned.1.call-start = ((), (), s32[]{:S(2)}) async-start(), calls=%async_computation.20 | async-start | bytes 540672
  709.1 2.7 collective-permute-start.10
  714.0 421.5 %reduce-scatter.15.cloned.1.call-start = ((), (), s32[]{:S(2)}) async-start(), calls=%async_computation.15 | async-start | bytes 3342336 | tf_op jit(solution)/shard_map/reduce_scatter | solution.py:255
  721.1 148.9 %copy-start.25 = (f32[64,1312]{1,0:T(8,128)S(1)}, f32[64,1312]{1,0:T(8,128)}, u32[]{:S(2)}) copy-start(f32[64,1312]{1,0:T(8,128)} %param.22) | copy-start | bytes 1007620
  784.2 88.3 %collective-permute-start.13 = (bf16[64,1312]{1,0:T(8,128)(2,1)}, bf16[64,1312]{1,0:T(8,128)(2,1)}, u32[]{:S(2)}, u32[]{:S(2)}) collective-permute-start(bf16[64,1312]{1,0:T(8,128)(2,1)} %get-tuple-element.140), channel_id=1, source_target_pairs={{0,1},{1,0},{2,3},{3,2},{4,5},{5,4},{6,7},{7,6},{8,9},{9,8},{10,11... | collective-permute-start | bytes 503816 | tf_op jit(solution)/shard_map/ppermute | solution.py:179
  876.0 260.5 %copy-start.43 = (f32[2,32]{1,0:T(2,128)S(1)}, f32[2,32]{1,0:T(2,128)}, u32[]{:S(2)}) copy-start(f32[2,32]{1,0:T(2,128)} %param.23) | copy-start | bytes 772
  876.0 261.8 %copy-start.23 = (f32[64,1536]{1,0:T(8,128)S(1)}, f32[64,1536]{1,0:T(8,128)}, u32[]{:S(2)}) copy-start(f32[64,1536]{1,0:T(8,128)} %param.19) | copy-start | bytes 1179652
  1136.4 1.4 collective-permute-start.11
  (48 other events, 532.5 us)
Sparse Core Ops, SparseCore 0:
  11.5 70.7 all-gather.6
  85.6 59.2 all-gather.8
  148.2 110.5 all-gather.10
  261.9 72.9 all-gather.12
  338.1 64.9 all-gather.14
  468.6 84.7 reduce-scatter.16
  555.8 138.3 reduce-scatter.20
  696.5 85.8 reduce-scatter.18
  784.8 85.1 reduce-scatter.22
  872.1 131.3 reduce-scatter.24
  1008.6 126.8 reduce-scatter.14

commit v2 on v1

--- a/solution.py
+++ b/solution.py
@@ -251,8 +251,40 @@
     def gather(shard):
         return lax.all_gather(shard, both, axis=0, tiled=True)
 
-    def scatter(grad):
-        return lax.psum_scatter(grad, both, scatter_dimension=0, tiled=True)
+    def begin(grad, high_first=False):
+        bits = {name: (lax.axis_size(name) - 1).bit_length() for name in both}
+        left = [(name, bit) for name in both for bit in reversed(range(bits[name]))]
+        steps = sorted(left, key=lambda at: (at[0] != "dp", at[1]))
+        if high_first:
+            steps = [at for at in left if at[0] == "dp"] + [at for at in steps if at[0] != "dp"]
+        rows = grad.shape[0] >> len(left)
+        return advance((grad.reshape((2,) * len(left) + (rows, grad.shape[1])), left, steps), 1)
+
+    def advance(state, count):
+        held, left, steps = state
+        left = list(left)
+        for name, bit in steps[:count]:
+            dim = left.index((name, bit))
+            left.pop(dim)
+            own = (lax.axis_index(name) >> bit) & 1
+            kept = lax.dynamic_index_in_dim(held, own, dim, keepdims=False)
+            sent = lax.dynamic_index_in_dim(held, 1 - own, dim, keepdims=False)
+            got = lax.ppermute(
+                sent.astype(jnp.bfloat16),
+                name,
+                [(at, at ^ (1 << bit)) for at in range(lax.axis_size(name))],
+            )
+            held = kept.astype(jnp.float32) + got.astype(jnp.float32)
+            if left:
+                held = held.astype(jnp.bfloat16)
+        return (held, left, steps[count:])
+
+    def scatter(state):
+        return advance(state, len(state[2]))[0]
+
+    def tie(value, states):
+        value, helds = lax.optimization_barrier((value, [state[0] for state in states]))
+        return value, [(held,) + state[1:] for held, state in zip(helds, states)]
 
     def with_other(rows):
         return jnp.concatenate([rows, swap(rows)], axis=0)
@@ -265,28 +297,29 @@
     low_qkv = w_qkv.astype(jnp.bfloat16)
     col_a, col_b, col_c = low_qkv[:, :third], low_qkv[:, third : 2 * third], low_qkv[:, 2 * third :]
     col_r = swap(col_b)
-    full_gain = lax.all_gather(
-        gains.astype(jnp.bfloat16), ("dp", "seq", "qblk"), axis=1, tiled=True
-    )
-    full_qkv = gather(
-        jnp.where(
-            first,
-            jnp.concatenate([col_a, col_c, col_r], axis=1),
-            jnp.concatenate([col_r, col_a, col_c], axis=1),
-        )
-    )
+    low_gain = gains.astype(jnp.bfloat16)
+    chip_gain = ordered(low_gain, swap(low_gain), 1).T
+    chip_gain = jnp.pad(chip_gain, ((0, 0), (0, 128 - gains.shape[0])))
+    shard_qkv = jnp.where(
+        first,
+        jnp.concatenate([col_a, col_c, col_r], axis=1),
+        jnp.concatenate([col_r, col_a, col_c], axis=1),
+    )
+    full_qkv = gather(jnp.concatenate([shard_qkv, chip_gain], axis=1))
     low_out = w_out.astype(jnp.bfloat16)
-    shard_out = ordered(low_out, swap(low_out), 1)
     low_in = w_in.astype(jnp.bfloat16)
     part = low_in.shape[1] // 2
     in_r = swap(jnp.where(first, low_in[:, part:], low_in[:, :part]))
     shard_gate = jnp.where(first, low_in[:, :part], in_r)
     shard_up = jnp.where(first, in_r, low_in[:, part:])
     low_ffn = w_ffn.astype(jnp.bfloat16)
-    full_qkv, shard_out, shard_gate, shard_up, low_ffn = lax.optimization_barrier(
-        (full_qkv, shard_out, shard_gate, shard_up, low_ffn)
-    )
-    full_out = gather(shard_out)
+    full_qkv, low_out, shard_gate, shard_up, low_ffn = lax.optimization_barrier(
+        (full_qkv, low_out, shard_gate, shard_up, low_ffn)
+    )
+    full_gain = full_qkv[:, 3 * third : 3 * third + gains.shape[0]].T
+    full_qkv = full_qkv[:, : 3 * third]
+    half_out = gather(low_out)
+    full_out = ordered(half_out, swap(half_out), 1)
     full_gate = gather(shard_gate)
     full_up = gather(shard_up)
     full_ffn = gather(low_ffn)
@@ -360,40 +393,45 @@
     heads_grad, grad_gate, grad_up, grad_ffn = lax.optimization_barrier(
         (heads_grad, grad_gate, grad_up, grad_ffn)
     )
-    sum_gate = scatter(grad_gate)
-    sum_up = scatter(grad_up)
-    sum_ffn = scatter(grad_ffn).astype(jnp.float32)
+    states = [begin(grad_gate), begin(grad_up, True), begin(grad_ffn)]
     grad_out = jnp.einsum("ft,td->fd", attn, mid_low, preferred_element_type=jnp.float32)
     out_cols = w_out.shape[1]
     out_mine = lax.dynamic_slice_in_dim(grad_out, core * out_cols, out_cols, axis=1)
     out_theirs = lax.dynamic_slice_in_dim(grad_out, (1 - core) * out_cols, out_cols, axis=1)
     out_sum = out_mine + swap(out_theirs.astype(jnp.bfloat16)).astype(jnp.float32)
-    sum_out = scatter(out_sum.astype(jnp.bfloat16)).astype(jnp.float32)
+    states.append(begin(out_sum.astype(jnp.bfloat16), True))
     block_part = times_t(hidden, full_ffn)
     block_out = (resid_mid + sum_own(block_part)).astype(jnp.bfloat16).reshape(tokens.shape)
 
     res = attend_back(qkv, cos_tab, sin_tab, head_out, lse, heads_grad[:, :, 0])
+    res, states = tie(res, states)
+    states = [advance(state, 1) for state in states]
     qkv_grad = from_heads(res, 3)
+    qkv_grad, states = tie(qkv_grad, states)
+    sum_gate, sum_up, sum_ffn, sum_out = [scatter(state) for state in states]
     grad_qkv = jnp.einsum("td,nt->dn", attn_in, qkv_grad, preferred_element_type=jnp.float32)
-    rows_qkv = scatter(grad_qkv.astype(jnp.bfloat16))
     in_grad = sum_own(
         jnp.einsum("nt,dn->td", qkv_grad, full_qkv, preferred_element_type=jnp.float32)
     )
     gain_one_grad = jnp.sum(in_grad * normed_one, axis=0)
     grad_x = mid_grad + norm_back(in_grad, normed_one, inv_one, gain_rows[0])
-    sum_gain = lax.psum_scatter(
-        jnp.stack([gain_one_grad, gain_two_grad]),
-        ("dp", "seq", "qblk"),
-        scatter_dimension=1,
-        tiled=True,
-    )
+    gain_cols = jnp.stack([gain_one_grad, gain_two_grad], axis=1)
+    gain_cols = jnp.pad(gain_cols, ((0, 0), (0, 128 - gain_cols.shape[1])))
+    low_rows = jnp.concatenate([grad_qkv, gain_cols], axis=1).astype(jnp.bfloat16)
+    rows_qkv = scatter(begin(low_rows))
+    gain_rows_sum = rows_qkv[:, 3 * third : 3 * third + gains.shape[0]].T
+    rows_qkv = rows_qkv[:, : 3 * third]
+    gain_wide = gains.shape[1]
+    gain_mine = lax.dynamic_slice_in_dim(gain_rows_sum, core * gain_wide, gain_wide, axis=1)
+    gain_theirs = lax.dynamic_slice_in_dim(gain_rows_sum, (1 - core) * gain_wide, gain_wide, axis=1)
+    sum_gain = gain_mine + swap(gain_theirs.astype(jnp.bfloat16)).astype(jnp.float32)
     q_sum, k_sum, v_sum = rows_qkv[:, :third], rows_qkv[:, third : 2 * third], rows_qkv[:, 2 * third :]
-    qkv_r = swap(jnp.where(first, v_sum, q_sum))
+    qkv_r = swap(jnp.where(first, v_sum, q_sum).astype(jnp.bfloat16)).astype(jnp.float32)
     sum_qkv = jnp.concatenate(
         [jnp.where(first, q_sum, k_sum), qkv_r, jnp.where(first, k_sum, v_sum)], axis=1
-    ).astype(jnp.float32)
-    gate_up_r = swap(jnp.where(first, sum_up, sum_gate))
-    sum_in = ordered(jnp.where(first, sum_gate, sum_up), gate_up_r, 1).astype(jnp.float32)
+    )
+    gate_up_r = swap(jnp.where(first, sum_up, sum_gate).astype(jnp.bfloat16)).astype(jnp.float32)
+    sum_in = ordered(jnp.where(first, sum_gate, sum_up), gate_up_r, 1)
     new_qkv = adam_step(
         w_qkv, sum_qkv, first_qkv, second_qkv, LR_FACTOR * D ** (-0.5), WEIGHT_DECAY
     )

time: 1150 us -> 870 us (0.76)
  waiting for transfers between devices: 778 us -> 429 us
  local copies, waits for them, and re-layouts: 66.2 us -> 123 us
  blocking collectives: 38.9 us -> 0 us
  other arithmetic: 50.8 us -> 75.4 us
  starting transfers between devices: 18.5 us -> 40.3 us
    reduce_scatter x5 -> x0, waiting for transfers between devices: 276 us -> none  [scatter(): return lax.psum_scatter(grad, both, scatter_dimension=0, tiled=True)]
    unnamed x12 -> x5, waiting for transfers between devices: 125 us -> 0.87 us
    ppermute x0 -> x20, waiting for transfers between devices: none -> 112 us  [advance(): lax.ppermute(sent.astype(jnp.bfloat16), name, [(at, at ^ 1 << bit) for at...]
    all_to_all x2, waiting for transfers between devices: 143 us -> 60.9 us  [from_heads(): back = lax.all_to_all(moved, 'seq', split_axis=0, concat_axis=0, tiled=True)]
    all_gather x5, waiting for transfers between devices: 127 us -> 167 us  [gather(): return lax.all_gather(shard, both, axis=0, tiled=True)]
    all_gather x1 -> x0, blocking collectives: 38.9 us -> none  [on_device(): lax.all_gather(gains.astype(jnp.bfloat16), ('dp', 'seq', 'qblk'), axis=1,...]
    convert_element_type x1 -> x21, other arithmetic: 1.34 us -> 27.8 us  [the longest x15 23.9 us: advance(): held = held.astype(jnp.bfloat16)]
    ppermute x0 -> x20, starting transfers between devices: none -> 21.5 us  [advance(): lax.ppermute(sent.astype(jnp.bfloat16), name, [(at, at ^ 1 << bit) for at...]
  transfers between devices with their start and end apart: 29 -> 45, of which waited for: 16 -> 24; matrix products, arithmetic and copies ran while one was open for 13% -> 21% of each run, Pallas kernels for 7% -> 10%
where the time goes in v2:
time: 870 us; the launch traced here: 860 us
  waiting for transfers between devices  429 us (49%)
  local copies, waits for them, and re-layouts  123 us (14%)
  matrix products  91.8 us (11%)
  Pallas kernels  85.9 us (10%)
  other arithmetic  75.4 us (9%)
  starting transfers between devices  40.3 us (5%)
  between operations  15.4 us (2%)
    all_gather x5, waiting for transfers between devices, gather(): return lax.all_gather(shard, both, axis=0, tiled=True)  167 us
    ppermute x20, waiting for transfers between devices, advance(): lax.ppermute(sent.astype(jnp.bfloat16), name, [(at, at ^ 1 << bit) for at...  112 us
    all_to_all x2, waiting for transfers between devices, to_heads(): return lax.all_to_all(split, 'seq', split_axis=0, concat_axis=0, tiled=True)  79.3 us
    all_to_all x2, waiting for transfers between devices, from_heads(): back = lax.all_to_all(moved, 'seq', split_axis=0, concat_axis=0, tiled=True)  60.9 us
    pallas_call x1, Pallas kernels, attend_back(): pl.pallas_call(attend_back_kernel, grid=(pairs,), in_specs=[pair_spec(par...  50.3 us
    pallas_call x1, Pallas kernels, attend(): pl.pallas_call(attend_kernel, grid=(pairs,), in_specs=[pair_spec(parts, 3...  35.6 us
    dot_general x3, matrix products, mm(): return jnp.dot(left, right, preferred_element_type=jnp.float32)  34.4 us
    convert_element_type x15, other arithmetic, advance(): held = held.astype(jnp.bfloat16)  23.9 us
  transfers between devices with their start and end apart: 45, of which 24 were waited for; matrix products, arithmetic and copies ran while one was open for 21% of the time, Pallas kernels for 10%

profile of v2, /device:TPU:0, one launch (start us, length us, event | category | flops | bytes accessed | tf_op | source)
XLA Modules:
  0.0 860.3 jit_solution(17037921037796912755)
XLA Ops:
  15.4 69.1 %all-gather.6.cloned.1.call-done = bf16[1024,1664]{1,0:T(8,128)(2,1)} async-done(((bf16[64,1664]{1,0:T(8,128)(2,1)}), bf16[1024,1664]{1,0:T(8,128)(2,1)}) %all-gather.6.cloned.1.call-update) | async-done | bytes 3407888 | tf_op jit(solution)/shard_map/all_gather | solution.py:252
  91.2 5.8 convolution_convert_fusion.4
  101.8 4.9 copy.210
  106.7 6.0 reshape.320
  118.8 75.5 %all-to-all-done.qkv_ref = bf16[4,4,3,64,512]{4,3,2,1,0:T(8,128)(2,1)S(1)} async-done(((bf16[4,4,3,64,512]{4,3,2,1,0:T(8,128)(2,1)}), bf16[4,4,3,64,512]{4,3,2,1,0:T(8,128)(2,1)S(1)}, u32[]{:S(2)}, u32[]{:S(2)}) %all-to-all-start) | async-done | bytes 3145760 | tf_op jit(solution)/shard_map/all_to_all | solution.py:340
  195.4 35.6 %attend.1 = (bf16[4,4,64,512]{3,2,1,0:T(8,128)(2,1)S(1)}, f32[4,4,1,512]{3,2,1,0:T(1,128)S(1)}) custom-call(bf16[4,4,3,64,512]{4,3,2,1,0:T(8,128)(2,1)S(1)} %all-to-all-done.qkv_ref, f32[4,32,512]{2,1,0:T(8,128)S(1)} %copy-done.3, f32[4,32,512]{2,1,0:T(8,128)S(1)} %get-tuple-element.207.sin_ref), custom_call_target="tpu_custom_call" | custom-call | flops 17179869184 | bytes 4194304 | tf_op jit(solution)/shard_map/attend/pallas_call | solution.py:117
  236.3 33.3 %all-to-all-done.1 = bf16[4,4,1,64,512]{4,3,1,2,0:T(8,128)(2,1)S(1)} async-done(((bf16[4,4,1,64,512]{4,3,1,2,0:T(8,128)(2,1)}), bf16[4,4,1,64,512]{4,3,1,2,0:T(8,128)(2,1)S(1)}, u32[]{:S(2)}, u32[]{:S(2)}) %all-to-all-start.1) | async-done | bytes 1048608 | tf_op jit(solution)/shard_map/all_to_all | solution.py:343
  285.0 7.8 fusion.75
  292.7 37.9 %all-gather.10.cloned.1.call-done = bf16[1024,1312]{1,0:T(8,128)(2,1)} async-done(((bf16[64,1312]{1,0:T(8,128)(2,1)}), bf16[1024,1312]{1,0:T(8,128)(2,1)}) %all-gather.10.cloned.1.call-update) | async-done | bytes 2686992 | tf_op jit(solution)/shard_map/all_gather | solution.py:252
  330.6 7.8 fusion.76
  338.4 60.3 %all-gather.14.cloned.1.call-done = bf16[1024,1312]{1,0:T(8,128)(2,1)} async-done(((bf16[64,1312]{1,0:T(8,128)(2,1)}), bf16[1024,1312]{1,0:T(8,128)(2,1)}) %all-gather.14.cloned.1.call-update) | async-done | bytes 2686992 | tf_op jit(solution)/shard_map/all_gather | solution.py:252
  398.8 18.9 %multiply_convert_fusion = (bf16[1024,1312]{0,1:T(8,128)(2,1)}, f32[1024,1312]{0,1:T(8,128)S(1)}, f32[1024,1312]{0,1:T(8,128)S(1)}) fusion(f32[1024,1312]{0,1:T(8,128)} %fusion.76, bf16[1024,1312]{1,0:T(8,128)(2,1)} %all-gather.14.cloned.1.call-done, bf16[512,1024]{1,0:T(8,128)(2,1)} %collective-permute-done.8, bf16[512,1024]{1,0:T(8,128)(2,1)S(1)} %bitcast.223), kind=kOutput, calls=%fused_computation.8 | convolution fusion | flops 2844327936 | bytes 23592960 | tf_op jit(solution)/shard_map/dot_general | solution.py:40
  417.6 12.8 %add_convert_fusion = (bf16[1024,1312]{0,1:T(8,128)(2,1)}, bf16[1024,1312]{0,1:T(8,128)(2,1)}) fusion(f32[1024,1312]{0,1:T(8,128)S(1)} %get-tuple-element.185, f32[1024,1312]{0,1:T(8,128)S(1)} %get-tuple-element.213, f32[1024,1312]{0,1:T(8,128)S(1)} %copy-done.24, f32[1024,1312]{0,1:T(8,128)S(1)} %copy-done.25), kind=kLoop, calls=%fused_computation.9 | loop fusion | flops 24182784 | bytes 26869760 | tf_op jit(solution)/shard_map/convert_element_type | solution.py:368
  430.5 6.3 fusion.87
  461.8 5.8 convolution_convert_fusion.1
  475.0 7.0 convolution_convert_fusion.2
  484.1 5.4 convolution_convert_fusion
  489.5 6.8 collective-permute-done.15
  526.8 50.3 %attend_back.1 = bf16[4,4,3,64,512]{4,3,2,1,0:T(8,128)(2,1)} custom-call(bf16[4,4,3,64,512]{4,3,2,1,0:T(8,128)(2,1)} %copy-done, f32[4,32,512]{2,1,0:T(8,128)S(1)} %copy-done.4, f32[4,32,512]{2,1,0:T(8,128)S(1)} %get-tuple-element.207.sin_ref, bf16[4,4,64,512]{3,2,1,0:T(8,128)(2,1)S(1)} %copy-done.2, f32[4,4,1,512]{3,2,1,0:T(1,128)S(1)} %get-tuple-element.44.lse_ref, ...), custom_call_target="tpu_custom_call" | custom-call | flops 42949672960 | bytes 10485760 | tf_op jit(solution)/shard_map/attend_back/pallas_call | solution.py:145
  605.1 11.8 %collective-permute-done.18 = bf16[2,2,64,1312]{3,2,1,0:T(8,128)(2,1)S(1)} collective-permute-done((bf16[2,2,64,1312]{3,2,1,0:T(8,128)(2,1)S(1)}, bf16[2,2,64,1312]{3,2,1,0:T(8,128)(2,1)S(1)}, u32[]{:S(2)}, u32[]{:S(2)}) %collective-permute-start.18) | collective-permute-done | bytes 671776 | tf_op jit(solution)/shard_map/ppermute | solution.py:272
  618.9 10.3 %collective-permute-done.16 = bf16[2,2,64,1312]{3,2,1,0:T(8,128)(2,1)S(1)} collective-permute-done((bf16[2,2,64,1312]{3,2,1,0:T(8,128)(2,1)S(1)}, bf16[2,2,64,1312]{3,2,1,0:T(8,128)(2,1)S(1)}, u32[]{:S(2)}, u32[]{:S(2)}) %collective-permute-start.16) | collective-permute-done | bytes 671776 | tf_op jit(solution)/shard_map/ppermute | solution.py:272
  630.2 27.5 %all-to-all-done.3 = bf16[4,4,3,64,512]{4,3,2,1,0:T(8,128)(2,1)S(1)} async-done(((bf16[4,4,3,64,512]{4,3,2,1,0:T(8,128)(2,1)}), bf16[4,4,3,64,512]{4,3,2,1,0:T(8,128)(2,1)S(1)}, u32[]{:S(2)}, u32[]{:S(2)}) %all-to-all-start.3) | async-done | bytes 3145760 | tf_op jit(solution)/shard_map/all_to_all | solution.py:343
  660.8 6.8 copy.209
  671.5 6.4 fusion.14
  681.1 5.3 convolution_convert_fusion.3
  686.4 6.8 copy.178
  698.6 9.6 %collective-permute-done.26 = bf16[2,64,512]{2,1,0:T(8,128)(2,1)S(1)} collective-permute-done((bf16[2,64,512]{2,1,0:T(8,128)(2,1)S(1)}, bf16[2,64,512]{2,1,0:T(8,128)(2,1)S(1)}, u32[]{:S(2)}, u32[]{:S(2)}) %collective-permute-start.26) | collective-permute-done | bytes 131104 | tf_op jit(solution)/shard_map/ppermute | solution.py:272
  742.9 8.3 collective-permute-done.29
  753.1 22.2 %collective-permute-done.21 = bf16[2,2,2,64,1664]{4,3,2,1,0:T(8,128)(2,1)} collective-permute-done((bf16[2,2,2,64,1664]{4,3,2,1,0:T(8,128)(2,1)}, bf16[2,2,2,64,1664]{4,3,2,1,0:T(8,128)(2,1)}, u32[]{:S(2)}, u32[]{:S(2)}) %collective-permute-start.21) | collective-permute-done | bytes 1703968 | tf_op jit(solution)/shard_map/ppermute | solution.py:272
  793.1 13.7 %collective-permute-done.22 = bf16[2,2,64,1664]{3,2,1,0:T(8,128)(2,1)} collective-permute-done((bf16[2,2,64,1664]{3,2,1,0:T(8,128)(2,1)}, bf16[2,2,64,1664]{3,2,1,0:T(8,128)(2,1)}, u32[]{:S(2)}, u32[]{:S(2)}) %collective-permute-start.22) | collective-permute-done | bytes 852000 | tf_op jit(solution)/shard_map/ppermute | solution.py:272
  815.5 9.6 %collective-permute-done.23 = bf16[2,64,1664]{2,1,0:T(8,128)(2,1)} collective-permute-done((bf16[2,64,1664]{2,1,0:T(8,128)(2,1)}, bf16[2,64,1664]{2,1,0:T(8,128)(2,1)}, u32[]{:S(2)}, u32[]{:S(2)}) %collective-permute-start.23) | collective-permute-done | bytes 426016 | tf_op jit(solution)/shard_map/ppermute | solution.py:272
  833.6 14.0 %collective-permute-done.24 = bf16[64,1664]{0,1:T(8,128)(2,1)S(1)} collective-permute-done((bf16[64,1664]{0,1:T(8,128)(2,1)S(1)}, bf16[64,1664]{0,1:T(8,128)(2,1)S(1)}, u32[]{:S(2)}, u32[]{:S(2)}) %collective-permute-start.24) | collective-permute-done | bytes 213024 | tf_op jit(solution)/shard_map/ppermute | solution.py:272
  (363 shorter events, 235.2 us)
Async XLA Ops:
  7.2 77.3 %all-gather.6.cloned.1.call-start = ((), (), s32[]{:S(2)}) async-start(), calls=%async_computation.4 | async-start | bytes 3620864 | tf_op jit(solution)/shard_map/all_gather | solution.py:252
  11.7 224.5 %all-gather.8.cloned.1.call-start = ((), (), s32[]{:S(2)}) async-start(), calls=%async_computation.5 | async-start | bytes 1114112 | tf_op jit(solution)/shard_map/all_gather | solution.py:252
  84.6 197.9 %all-gather.12.cloned.1.call-start = ((), (), s32[]{:S(2)}) async-start(), calls=%async_computation.7 | async-start | bytes 3063808 | tf_op jit(solution)/shard_map/all_gather | solution.py:252
  112.7 81.6 %all-to-all-start = ((bf16[4,4,3,64,512]{4,3,2,1,0:T(8,128)(2,1)}), bf16[4,4,3,64,512]{4,3,2,1,0:T(8,128)(2,1)S(1)}, u32[]{:S(2)}, u32[]{:S(2)}) async-start(bf16[4,4,3,64,512]{4,3,2,1,0:T(8,128)(2,1)} %reshape.320), calls=%async_computation | async-start | bytes 6291456 | tf_op jit(solution)/shard_map/all_to_all | solution.py:340
  116.4 214.2 %all-gather.10.cloned.1.call-start = ((), (), s32[]{:S(2)}) async-start(), calls=%async_computation.6 | async-start | bytes 3063808 | tf_op jit(solution)/shard_map/all_gather | solution.py:252
  232.1 37.6 %all-to-all-start.1 = ((bf16[4,4,1,64,512]{4,3,1,2,0:T(8,128)(2,1)}), bf16[4,4,1,64,512]{4,3,1,2,0:T(8,128)(2,1)S(1)}, u32[]{:S(2)}, u32[]{:S(2)}) async-start(bf16[4,4,1,64,512]{4,3,1,2,0:T(8,128)(2,1)} %bitcast.207), calls=%async_computation.1 | async-start | bytes 2097152 | tf_op jit(solution)/shard_map/all_to_all | solution.py:343
  235.6 163.2 %all-gather.14.cloned.1.call-start = ((), (), s32[]{:S(2)}) async-start(), calls=%async_computation.8 | async-start | bytes 3063808 | tf_op jit(solution)/shard_map/all_gather | solution.py:252
  236.2 38.3 %collective-permute-start.5 = (bf16[1024,512]{1,0:T(8,128)(2,1)}, bf16[1024,512]{1,0:T(8,128)(2,1)}, u32[]{:S(2)}, u32[]{:S(2)}) collective-permute-start(bf16[1024,512]{1,0:T(8,128)(2,1)} %all-gather.8.cloned.1.call-done), channel_id=1, source_target_pairs={{0,1},{1,0},{2,3},{3,2},{4,5},{5,4},{6,7},{7,6},{8,9},{9,8},{10,11... | collective-permute-start | bytes 3145736 | tf_op jit(solution)/shard_map/ppermute | solution.py:179
  282.1 56.3 %collective-permute-start.8 = (bf16[512,1024]{1,0:T(8,128)(2,1)S(1)}, bf16[512,1024]{1,0:T(8,128)(2,1)}, u32[]{:S(2)}, u32[]{:S(2)}) collective-permute-start(bf16[512,1024]{1,0:T(8,128)(2,1)S(1)} %bitcast.222), channel_id=1, source_target_pairs={{0,1},{1,0},{2,3},{3,2},{4,5},{5,4},{6,7},{7,6},{8,9},{9,8},{10,11... | collective-permute-start | bytes 3145736 | tf_op jit(solution)/shard_map/ppermute | solution.py:179
  457.5 24.5 %collective-permute-start.14 = (bf16[1024,512]{1,0:T(8,128)(2,1)}, bf16[1024,512]{1,0:T(8,128)(2,1)S(1)}, u32[]{:S(2)}, u32[]{:S(2)}) collective-permute-start(bf16[1024,512]{1,0:T(8,128)(2,1)} %dynamic-slice_convert_fusion), channel_id=1, source_target_pairs={{0,1},{1,0},{2,3},{3,2},{4,5},{5,4},{6,7},{7,6},{8,9},{9,8},{10,11... | collective-permute-start | bytes 3145736 | tf_op jit(solution)/shard_map/ppermute | solution.py:179
  471.4 29.7 %all-to-all-start.2 = ((bf16[4,4,1,64,512]{4,3,1,2,0:T(8,128)(2,1)}), bf16[4,4,1,64,512]{4,3,1,2,0:T(8,128)(2,1)S(1)}, u32[]{:S(2)}, u32[]{:S(2)}) async-start(bf16[4,4,1,64,512]{4,3,1,2,0:T(8,128)(2,1)} %bitcast.10), calls=%async_computation.2 | async-start | bytes 2097152 | tf_op jit(solution)/shard_map/all_to_all | solution.py:340
  482.6 13.8 %collective-permute-start.15 = (bf16[2,2,2,64,512]{4,3,1,2,0:T(8,128)(2,1)S(1)}, bf16[2,2,2,64,512]{4,3,1,2,0:T(8,128)(2,1)S(1)}, u32[]{:S(2)}, u32[]{:S(2)}) collective-permute-start(bf16[2,2,2,64,512]{4,3,1,2,0:T(8,128)(2,1)S(1)} %bitcast.228), channel_id=1, source_target_pairs={{0,16},{8,24},{16,0},{24,8},{1,17},{9,25},{17,1},{25,9},{2,18},{10... | collective-permute-start | bytes 1572872 | tf_op jit(solution)/shard_map/ppermute | solution.py:272
  508.2 68.9 %collective-permute-start.13 = (bf16[2,2,2,64,1312]{4,3,2,1,0:T(8,128)(2,1)}, bf16[2,2,2,64,1312]{4,3,2,1,0:T(8,128)(2,1)}, u32[]{:S(2)}, u32[]{:S(2)}) collective-permute-start(bf16[2,2,2,64,1312]{4,3,2,1,0:T(8,128)(2,1)} %dynamic-slice_bitcast_fusion), channel_id=1, source_target_pairs={{0,8},{8,0},{16,24},{24,16},{1,9},{9,1},{17,25},{25,17},{2,10},{10... | collective-permute-start | bytes 4030472 | tf_op jit(solution)/shard_map/ppermute | solution.py:272
  518.4 63.1 %collective-permute-start.12 = (bf16[2,2,2,64,1312]{4,3,1,2,0:T(8,128)(2,1)}, bf16[2,2,2,64,1312]{4,3,1,2,0:T(8,128)(2,1)}, u32[]{:S(2)}, u32[]{:S(2)}) collective-permute-start(bf16[2,2,2,64,1312]{4,3,1,2,0:T(8,128)(2,1)} %bitcast.204), channel_id=1, source_target_pairs={{0,16},{8,24},{16,0},{24,8},{1,17},{9,25},{17,1},{25,9},{2,18},{10... | collective-permute-start | bytes 4030472 | tf_op jit(solution)/shard_map/ppermute | solution.py:272
  525.3 54.9 %collective-permute-start.11 = (bf16[2,2,2,64,1312]{4,3,2,1,0:T(8,128)(2,1)S(1)}, bf16[2,2,2,64,1312]{4,3,2,1,0:T(8,128)(2,1)S(1)}, u32[]{:S(2)}, u32[]{:S(2)}) collective-permute-start(bf16[2,2,2,64,1312]{4,3,2,1,0:T(8,128)(2,1)S(1)} %dynamic-slice_bitcast_fusion.1), channel_id=1, source_target_pairs={{0,8},{8,0},{16,24},{24,16},{1,9},{9,1},{17,25},{25,17},{2,10},{10... | collective-permute-start | bytes 4030472 | tf_op jit(solution)/shard_map/ppermute | solution.py:272
  584.4 73.3 %all-to-all-start.3 = ((bf16[4,4,3,64,512]{4,3,2,1,0:T(8,128)(2,1)}), bf16[4,4,3,64,512]{4,3,2,1,0:T(8,128)(2,1)S(1)}, u32[]{:S(2)}, u32[]{:S(2)}) async-start(bf16[4,4,3,64,512]{4,3,2,1,0:T(8,128)(2,1)} %attend_back.1), calls=%async_computation.3 | async-start | bytes 6291456 | tf_op jit(solution)/shard_map/all_to_all | solution.py:343
  597.7 19.1 %collective-permute-start.18 = (bf16[2,2,64,1312]{3,2,1,0:T(8,128)(2,1)S(1)}, bf16[2,2,64,1312]{3,2,1,0:T(8,128)(2,1)S(1)}, u32[]{:S(2)}, u32[]{:S(2)}) collective-permute-start(bf16[2,2,64,1312]{3,2,1,0:T(8,128)(2,1)S(1)} %dynamic-slice_bitcast_fusion.2), channel_id=1, source_target_pairs={{0,16},{8,24},{16,0},{24,8},{1,17},{9,25},{17,1},{25,9},{2,18},{10... | collective-permute-start | bytes 2015240 | tf_op jit(solution)/shard_map/ppermute | solution.py:272
  600.2 17.7 %collective-permute-start.17 = (bf16[2,2,64,1312]{3,2,0,1:T(8,128)(2,1)S(1)}, bf16[2,2,64,1312]{3,2,0,1:T(8,128)(2,1)S(1)}, u32[]{:S(2)}, u32[]{:S(2)}) collective-permute-start(bf16[2,2,64,1312]{3,2,0,1:T(8,128)(2,1)S(1)} %dynamic-slice_bitcast_fusion.3), channel_id=1, source_target_pairs={{0,8},{8,0},{16,24},{24,16},{1,9},{9,1},{17,25},{25,17},{2,10},{10... | collective-permute-start | bytes 2015240 | tf_op jit(solution)/shard_map/ppermute | solution.py:272
  601.0 28.2 %collective-permute-start.16 = (bf16[2,2,64,1312]{3,2,1,0:T(8,128)(2,1)S(1)}, bf16[2,2,64,1312]{3,2,1,0:T(8,128)(2,1)S(1)}, u32[]{:S(2)}, u32[]{:S(2)}) collective-permute-start(bf16[2,2,64,1312]{3,2,1,0:T(8,128)(2,1)S(1)} %dynamic-slice_bitcast_fusion.4), channel_id=1, source_target_pairs={{0,16},{8,24},{16,0},{24,8},{1,17},{9,25},{17,1},{25,9},{2,18},{10... | collective-permute-start | bytes 2015240 | tf_op jit(solution)/shard_map/ppermute | solution.py:272
  681.1 40.9 %collective-permute-start.20 = (bf16[512,1024]{1,0:T(8,128)(2,1)}, bf16[512,1024]{1,0:T(8,128)(2,1)S(1)}, u32[]{:S(2)}, u32[]{:S(2)}) collective-permute-start(bf16[512,1024]{1,0:T(8,128)(2,1)} %slice.157), channel_id=1, source_target_pairs={{0,1},{1,0},{2,3},{3,2},{4,5},{5,4},{6,7},{7,6},{8,9},{9,8},{10,11... | collective-permute-start | bytes 3145736 | tf_op jit(solution)/shard_map/ppermute | solution.py:179
  694.0 44.2 %collective-permute-start.33 = (bf16[2,64,1312]{2,1,0:T(8,128)(2,1)}, bf16[2,64,1312]{2,1,0:T(8,128)(2,1)}, u32[]{:S(2)}, u32[]{:S(2)}) collective-permute-start(bf16[2,64,1312]{2,1,0:T(8,128)(2,1)} %dynamic-slice_bitcast_fusion.6), channel_id=1, source_target_pairs={{0,2},{2,0},{4,6},{6,4},{1,3},{3,1},{5,7},{7,5},{8,10},{10,8},{12,... | collective-permute-start | bytes 1007624 | tf_op jit(solution)/shard_map/ppermute | solution.py:272
  695.4 12.8 %collective-permute-start.26 = (bf16[2,64,512]{2,1,0:T(8,128)(2,1)S(1)}, bf16[2,64,512]{2,1,0:T(8,128)(2,1)S(1)}, u32[]{:S(2)}, u32[]{:S(2)}) collective-permute-start(bf16[2,64,512]{2,1,0:T(8,128)(2,1)S(1)} %dynamic-slice_bitcast_fusion.13), channel_id=1, source_target_pairs={{0,2},{2,0},{4,6},{6,4},{1,3},{3,1},{5,7},{7,5},{8,10},{10,8},{12,... | collective-permute-start | bytes 393224 | tf_op jit(solution)/shard_map/ppermute | solution.py:272
  698.0 19.3 %collective-permute-start.30 = (bf16[2,64,1312]{2,1,0:T(8,128)(2,1)S(1)}, bf16[2,64,1312]{2,1,0:T(8,128)(2,1)S(1)}, u32[]{:S(2)}, u32[]{:S(2)}) collective-permute-start(bf16[2,64,1312]{2,1,0:T(8,128)(2,1)S(1)} %dynamic-slice_bitcast_fusion.7), channel_id=1, source_target_pairs={{0,2},{2,0},{4,6},{6,4},{1,3},{3,1},{5,7},{7,5},{8,10},{10,8},{12,... | collective-permute-start | bytes 1007624 | tf_op jit(solution)/shard_map/ppermute | solution.py:272
  710.0 26.9 %collective-permute-start.28 = (bf16[2,64,1312]{2,1,0:T(8,128)(2,1)}, bf16[2,64,1312]{2,1,0:T(8,128)(2,1)}, u32[]{:S(2)}, u32[]{:S(2)}) collective-permute-start(bf16[2,64,1312]{2,1,0:T(8,128)(2,1)} %dynamic-slice_bitcast_fusion.8), channel_id=1, source_target_pairs={{0,2},{2,0},{4,6},{6,4},{1,3},{3,1},{5,7},{7,5},{8,10},{10,8},{12,... | collective-permute-start | bytes 1007624 | tf_op jit(solution)/shard_map/ppermute | solution.py:272
  719.2 23.7 %collective-permute-start.31 = (bf16[64,1312]{1,0:T(8,128)(2,1)}, bf16[64,1312]{1,0:T(8,128)(2,1)}, u32[]{:S(2)}, u32[]{:S(2)}) collective-permute-start(bf16[64,1312]{1,0:T(8,128)(2,1)} %dynamic-slice_bitcast_fusion.11), channel_id=1, source_target_pairs={{0,4},{2,6},{4,0},{6,2},{1,5},{3,7},{5,1},{7,3},{8,12},{10,14},{12... | collective-permute-start | bytes 503816 | tf_op jit(solution)/shard_map/ppermute | solution.py:272
  736.4 38.9 %collective-permute-start.21 = (bf16[2,2,2,64,1664]{4,3,2,1,0:T(8,128)(2,1)}, bf16[2,2,2,64,1664]{4,3,2,1,0:T(8,128)(2,1)}, u32[]{:S(2)}, u32[]{:S(2)}) collective-permute-start(bf16[2,2,2,64,1664]{4,3,2,1,0:T(8,128)(2,1)} %bitcast.221), channel_id=1, source_target_pairs={{0,8},{8,0},{16,24},{24,16},{1,9},{9,1},{17,25},{25,17},{2,10},{10... | collective-permute-start | bytes 5111816 | tf_op jit(solution)/shard_map/ppermute | solution.py:272
  738.0 13.2 %collective-permute-start.29 = (bf16[64,1312]{1,0:T(8,128)(2,1)S(1)}, bf16[64,1312]{1,0:T(8,128)(2,1)S(1)}, u32[]{:S(2)}, u32[]{:S(2)}) collective-permute-start(bf16[64,1312]{1,0:T(8,128)(2,1)S(1)} %dynamic-slice_bitcast_fusion.12), channel_id=1, source_target_pairs={{0,4},{2,6},{4,0},{6,2},{1,5},{3,7},{5,1},{7,3},{8,12},{10,14},{12... | collective-permute-start | bytes 503816 | tf_op jit(solution)/shard_map/ppermute | solution.py:272
  740.0 47.8 %collective-permute-start.34 = (bf16[64,1312]{1,0:T(8,128)(2,1)}, bf16[64,1312]{1,0:T(8,128)(2,1)}, u32[]{:S(2)}, u32[]{:S(2)}) collective-permute-start(bf16[64,1312]{1,0:T(8,128)(2,1)} %dynamic-slice_bitcast_fusion.10), channel_id=1, source_target_pairs={{0,4},{2,6},{4,0},{6,2},{1,5},{3,7},{5,1},{7,3},{8,12},{10,14},{12... | collective-permute-start | bytes 503816 | tf_op jit(solution)/shard_map/ppermute | solution.py:272
  753.0 37.3 %collective-permute-start.32 = (bf16[64,1312]{1,0:T(8,128)(2,1)}, bf16[64,1312]{1,0:T(8,128)(2,1)}, u32[]{:S(2)}, u32[]{:S(2)}) collective-permute-start(bf16[64,1312]{1,0:T(8,128)(2,1)} %get-tuple-element.192), channel_id=1, source_target_pairs={{0,1},{1,0},{2,3},{3,2},{4,5},{5,4},{6,7},{7,6},{8,9},{9,8},{10,11... | collective-permute-start | bytes 503816 | tf_op jit(solution)/shard_map/ppermute | solution.py:179
  787.2 19.7 %collective-permute-start.22 = (bf16[2,2,64,1664]{3,2,1,0:T(8,128)(2,1)}, bf16[2,2,64,1664]{3,2,1,0:T(8,128)(2,1)}, u32[]{:S(2)}, u32[]{:S(2)}) collective-permute-start(bf16[2,2,64,1664]{3,2,1,0:T(8,128)(2,1)} %bitcast.227), channel_id=1, source_target_pairs={{0,16},{8,24},{16,0},{24,8},{1,17},{9,25},{17,1},{25,9},{2,18},{10... | collective-permute-start | bytes 2555912 | tf_op jit(solution)/shard_map/ppermute | solution.py:272
  815.4 9.6 %collective-permute-start.23 = (bf16[2,64,1664]{2,1,0:T(8,128)(2,1)}, bf16[2,64,1664]{2,1,0:T(8,128)(2,1)}, u32[]{:S(2)}, u32[]{:S(2)}) collective-permute-start(bf16[2,64,1664]{2,1,0:T(8,128)(2,1)} %bitcast.229), channel_id=1, source_target_pairs={{0,2},{2,0},{4,6},{6,4},{1,3},{3,1},{5,7},{7,5},{8,10},{10,8},{12,... | collective-permute-start | bytes 1277960 | tf_op jit(solution)/shard_map/ppermute | solution.py:272
  829.1 18.5 %collective-permute-start.24 = (bf16[64,1664]{0,1:T(8,128)(2,1)S(1)}, bf16[64,1664]{0,1:T(8,128)(2,1)S(1)}, u32[]{:S(2)}, u32[]{:S(2)}) collective-permute-start(bf16[64,1664]{0,1:T(8,128)(2,1)S(1)} %dynamic-slice_bitcast_fusion.5), channel_id=1, source_target_pairs={{0,4},{2,6},{4,0},{6,2},{1,5},{3,7},{5,1},{7,3},{8,12},{10,14},{12... | collective-permute-start | bytes 638984 | tf_op jit(solution)/shard_map/ppermute | solution.py:272
  (90 other events, 855.1 us)
Sparse Core Ops, SparseCore 0:
  11.8 72.6 all-gather.5
  87.9 89.9 all-gather.7
  181.2 76.3 all-gather.11
  260.7 69.8 all-gather.9
  333.7 64.9 all-gather.13
